TPU v7x, 32 devices: a whole 2x2x4 slice. The times are simulated.
32 devices in a mesh: dp: 2 (over core), row: 4 (over z), col: 4 (over y, x).
Axes of the slice: x: 2, y: 2, z: 4, core: 2. Of those that a mesh axis runs over, the one named last changes fastest.
Arguments:
- inputs: bfloat16 [1024, 6144], P(('dp', 'row'), 'col'), may hold values from -6 to 6
- up_weight: bfloat16 [6144, 24576], P('col', ('dp', 'row')), may hold values from -0.078125 to 0.078125
- down_weight: bfloat16 [24576, 6144], P(('dp', 'row'), 'col'), may hold values from -0.0390625 to 0.0390625
- cotangent: bfloat16 [1024, 6144], P(('dp', 'row'), 'col'), may hold values from -3 to 3
Outputs:
- input_grad: bfloat16 [1024, 6144], P(('dp', 'row'), 'col')
- up_grad: bfloat16 [6144, 24576], P('col', ('dp', 'row'))
- down_grad: bfloat16 [24576, 6144], P(('dp', 'row'), 'col')
All inputs are finite; a program needn't handle non-finite values.
Results may differ from a plain program's by a relative error of at most 0.0049.
Values may be sent and summed in bfloat16 or wider, within the bound.
No kernel may reach another device: no remote copies, remote signals or barrier semaphores. Data moves between devices by JAX's collectives and lax.ppermute only.
A program may use at most 128 MiB of HBM per device.

v0:
```python
import math

import jax
import jax.numpy as jnp
from jax import lax
from jax.experimental import pallas as pl
from jax.experimental.pallas import tpu as pltpu
from jax.sharding import PartitionSpec as P

gelu_const = math.sqrt(2.0 / math.pi)
f32, b16 = jnp.float32, jnp.bfloat16
FIRST_SUM, ODD_JOIN = 14_000_000_000, 12_000_000_000


def gelu_both(value):
    square = value * value
    tangent = jnp.tanh(gelu_const * (value + 0.044715 * square * value))
    half = 0.5 * (1.0 + tangent)
    slope = half + 0.5 * value * (1.0 - tangent * tangent) * gelu_const * (1.0 + 3.0 * 0.044715 * square)
    return value * half, slope


def contract(left, right, at_left, at_right):
    return lax.dot_general(
        left, right, (((at_left,), (at_right,)), ((), ())), preferred_element_type=f32
    )


def call(body, operands, in_specs, outs, out_specs, grid, name, limit=4 * 2**20, flops=1000, scratch=()):
    return pl.pallas_call(
        body,
        grid=grid,
        in_specs=in_specs,
        out_specs=out_specs,
        out_shape=outs,
        scratch_shapes=list(scratch),
        compiler_params=pltpu.CompilerParams(vmem_limit_bytes=limit),
        cost_estimate=pl.CostEstimate(flops=flops, bytes_accessed=1000, transcendentals=0),
        name=name,
    )(*operands)


def shape(dims, dtype):
    return jax.ShapeDtypeStruct(dims, dtype)


def tile_of(size, most):
    return max(t for t in range(128, most + 1, 128) if size % t == 0)


whole = pl.BlockSpec(memory_space=pltpu.VMEM)


def cut_of(hidden):
    return hidden // 256 * 128


def first_product(chunk, weight, weight_dim, cut, name):
    tokens = chunk.shape[0]
    hidden = weight.shape[1 - weight_dim]
    half, quarter = tokens // 2, tokens // 4
    widths = [cut] + [hidden - cut] * (cut < hidden)

    def body(chunk_ref, weight_ref, kept_ref, *sent_refs):
        for start in range(0, hidden, tile_of(hidden, 512) if cut == hidden else 128 if cut % 512 else 512):
            tile = min(hidden, start + (tile_of(hidden, 512) if cut == hidden else 128 if cut % 512 else 512)) - start
            span = pl.ds(start, tile)
            block = weight_ref[:, span] if weight_dim == 0 else weight_ref[span, :]
            total = contract(chunk_ref[...], block, 1, weight_dim)
            if start < cut:
                kept, sent = total[:half], total[half:]
            else:
                q = [total[i * quarter : (i + 1) * quarter] for i in range(4)]
                kept, sent = jnp.concatenate([q[0], q[2]], axis=0), jnp.concatenate([q[1], q[3]], axis=0)
            kept_ref[:, span] = kept
            sent_refs[start >= cut][:, pl.ds(start - cut * (start >= cut), tile)] = sent.astype(b16)

    return call(
        body,
        [chunk, weight],
        [whole] * 2,
        [shape((half, hidden), f32)] + [shape((half, w), b16) for w in widths],
        [whole] * (1 + len(widths)),
        (),
        name,
    )


def add_halves(kept_h, came_h, kept_g, came_g, flops):
    tokens, hidden = kept_h.shape
    half = tokens // 2
    tile = tile_of(hidden, 768)

    def body(kh, ch, kg, cg, sent_h, next_h, sent_g, next_g):
        for kept, came, sent, rest in ((kh, ch, sent_h, next_h), (kg, cg, sent_g, next_g)):
            total = kept[...] + came[...].astype(f32)
            rest[...] = total[:half]
            sent[...] = total[half:].astype(b16)

    block = pl.BlockSpec((tokens, tile), lambda i: (0, i))
    part = pl.BlockSpec((half, tile), lambda i: (0, i))
    return call(
        body,
        [kept_h, came_h, kept_g, came_g],
        [block] * 4,
        [shape((half, hidden), b16), shape((half, hidden), f32)] * 2,
        [part] * 4,
        (hidden // tile,),
        "add_halves",
        flops=flops,
    )


def add_crossed(kept_h, came_h, kept_g, came_g, cut, flops):
    tokens, hidden = kept_h.shape
    half = tokens // 2

    def body(kh, h0, h1, kg, g0, g1, sent_hg, next_h, sent_gh, next_g):
        for kept, came, rest, sents in ((kh, (h0, h1), next_h, (sent_hg, sent_gh)), (kg, (g0, g1), next_g, (sent_gh, sent_hg))):
            for side in range(2):
                span = pl.ds(cut * side, (cut, hidden - cut)[side])
                total = kept[:, span] + came[side][...].astype(f32)
                rest[:, span] = total[:half]
                sents[side][:, span] = total[half:].astype(b16)

    return call(
        body,
        [kept_h, *came_h, kept_g, *came_g],
        [whole] * 6,
        [shape((half, hidden), b16), shape((half, hidden), f32)] * 2,
        [whole] * 4,
        (),
        "add_crossed",
        flops=flops,
    )


def activate(kept_h, came_h, kept_g, came_g, cut):
    tokens, hidden = kept_h.shape
    tile = tile_of(cut, 768) if hidden % cut == 0 else 128

    def body(kh, ch, kg, cg, active_ref, delta_ref):
        came_h, came_g = ch[...].astype(f32), cg[...].astype(f32)
        if cut < hidden:
            straight = pl.program_id(0) < cut // tile
            came_h, came_g = jnp.where(straight, came_h, came_g), jnp.where(straight, came_g, came_h)
        value, slope = gelu_both(kh[...] + came_h)
        active_ref[...] = value.astype(b16)
        delta_ref[...] = ((kg[...] + came_g) * slope).astype(b16)

    block = pl.BlockSpec((tokens, tile), lambda i: (0, i))
    return call(
        body, [kept_h, came_h, kept_g, came_g], [block] * 4, [shape((tokens, hidden), b16)] * 2, [block] * 2,
        (hidden // tile,), "activate",
    )


def join_pairs(flops, *arrays):
    rows, columns = arrays[0].shape
    tile = tile_of(columns, 1536)

    def body(*refs):
        for i, out in enumerate(refs[len(arrays):]):
            out[pl.ds(0, rows), :] = refs[2 * i][...]
            out[pl.ds(rows, rows), :] = refs[2 * i + 1][...]

    return call(
        body,
        arrays,
        [pl.BlockSpec((rows, tile), lambda i: (0, i))] * len(arrays),
        [shape((2 * rows, columns), arrays[0].dtype)] * (len(arrays) // 2),
        [pl.BlockSpec((2 * rows, tile), lambda i: (0, i))] * (len(arrays) // 2),
        (columns // tile,),
        "join_pairs",
        7 * 2**20,
        flops,
    )


def input_product(delta, up_weight, quarter, cuts):
    tokens = delta.shape[0]
    width = up_weight.shape[0]
    tile = tile_of(width, 512)
    pairs = tokens // (2 * quarter)

    def body(delta_ref, weight_ref, kept_ref, *sent_refs):
        for start in range(0, width, tile):
            span = pl.ds(start, tile)
            total = contract(delta_ref[...], weight_ref[span, :], 1, 1)
            for i in range(pairs):
                first, second = 2 * i * quarter, (2 * i + 1) * quarter
                kept_ref[pl.ds(i * quarter, quarter), span] = total[first:second]
                sent_ref = sent_refs[cuts * i // pairs]
                sent_ref[pl.ds(i % (pairs // cuts) * quarter, quarter), span] = total[second : second + quarter]

    outs = [shape((tokens // 2, width), f32)] + [shape((tokens // (2 * cuts), width), f32)] * cuts
    return call(body, [delta, up_weight], [whole] * 2, outs, [whole] * (1 + cuts), (), "input_product")


def add_shares(kept_ref, *rest):
    total, cut = kept_ref[...], kept_ref.shape[0] // 2
    while rest:
        if rest[0].shape[0] == cut:
            total = total + jnp.concatenate([rest[0][...], rest[1][...]], axis=0)
            rest = rest[2:]
        else:
            total = total + rest[0][...].astype(f32)
            rest = rest[1:]
    return total


def steps_of(*sizes):
    return max(n for n in range(1, 7) if all(size % (128 * n) == 0 for size in sizes))


def weight_total(lefts, rights, columns):
    total = contract(lefts[0][:, columns], rights[0][...], 0, 0)
    for left, right in zip(lefts[1:], rights[1:]):
        total = total + contract(left[:, columns], right[...], 0, 0)
    return total


def early_grad(lefts, rights, held, name):
    rows, columns = lefts[0].shape[1], rights[0].shape[1]
    steps = steps_of(rows)
    tile = rows // steps
    count = len(lefts)

    def body(*refs):
        mine = pl.ds(pl.multiple_of(pl.program_id(0) * tile, tile), tile)
        total = weight_total(refs[:count], refs[count:-1], mine)
        if held:
            refs[-1][mine, :] = total
        else:
            refs[-1][...] = total

    return call(
        body,
        [*lefts, *rights],
        [whole] * (2 * count),
        shape((rows, columns), f32) if held else pltpu.HBM((rows, columns), f32),
        whole if held else pl.BlockSpec((tile, columns), lambda i: (i, 0)),
        (steps,),
        name,
        10 * 2**20,
    )


def late_grad(lefts, rights, partial, held, scale, name):
    rows, columns = partial.shape
    steps = steps_of(rows)
    tile = rows // steps
    count = len(lefts)

    def body(*refs):
        mine = pl.ds(pl.multiple_of(pl.program_id(0) * tile, tile), tile)
        total = weight_total(refs[:count], refs[count : 2 * count], mine)
        total = total + (refs[-2][mine, :] if held else refs[-2][...])
        refs[-1][...] = (total * scale).astype(b16)

    block = pl.BlockSpec((tile, columns), lambda i: (i, 0))
    return call(
        body,
        [*lefts, *rights, partial],
        [whole] * (2 * count) + [whole if held else block],
        pltpu.HBM((rows, columns), b16),
        block,
        (steps,),
        name,
        8 * 2**20,
    )


def shards(inputs, up_weight, down_weight, cotangent):
    n_row = lax.axis_size("row")
    replicas = lax.axis_size("dp")
    n_col = lax.axis_size("col")
    assert replicas == 2 and n_col == 4 and n_row % 4 == 0
    rows, width = inputs.shape
    quarter = rows // n_col
    own = lax.axis_index("col")

    def swap_x(a):
        return lax.ppermute(a, "col", [(i, i ^ 1) for i in range(n_col)])

    def swap_y(a):
        return lax.ppermute(a, "col", [(i, i ^ 2) for i in range(n_col)])

    def swap_dp(a):
        return lax.ppermute(a, "dp", [(0, 1), (1, 0)])

    def pass_row(a):
        return lax.ppermute(a, "row", [(i, (i + 1) % n_row) for i in range(n_row)])

    def reorder(a, order):
        blocks = [lax.dynamic_slice_in_dim(a, (own ^ bits) * quarter, quarter, 0) for bits in order]
        return jnp.concatenate(blocks, axis=0)

    x_outer, y_outer = (0, 2, 1, 3), (0, 1, 2, 3)

    def reorder_both():
        def body(own_ref, inputs_ref, cotangent_ref, out_ref, done):
            copies = []
            for ref, order, base in ((inputs_ref, x_outer, 0), (cotangent_ref, y_outer, rows)):
                for i in range(n_col):
                    source = pl.multiple_of((own_ref[0] ^ order[i]) * quarter, quarter)
                    copies.append(
                        pltpu.make_async_copy(
                            ref.at[pl.ds(source, quarter), :],
                            out_ref.at[pl.ds(base + i * quarter, quarter), :],
                            done.at[len(copies)],
                        )
                    )
            for copy in copies:
                copy.start()
            for copy in copies:
                copy.wait()

        return call(
            body,
            [own.astype(jnp.int32).reshape(1)]
            + [pltpu.with_memory_space_constraint(a, pltpu.HBM) for a in (inputs, cotangent)],
            [pl.BlockSpec(memory_space=pltpu.SMEM)] + [pl.BlockSpec(memory_space=pltpu.HBM)] * 2,
            shape((2 * rows, width), b16),
            whole,
            (),
            "reorder",
            scratch=[pltpu.SemaphoreType.DMA((2 * n_col,))],
        )

    if quarter % 16 == 0:
        moving = reorder_both()
    else:
        moving = jnp.concatenate([reorder(inputs, x_outer), reorder(cotangent, y_outer)], axis=0)

    group = n_row // 4
    tall = group * rows
    work = [{} for _ in range(4)]
    blocks = {0: [moving]}
    aligned = group == 1 and quarter % 16 == 0

    token = ()

    def after(*values):
        tied = lax.optimization_barrier((*values, *token))[: len(values)]
        return tied if len(values) > 1 else tied[0]

    def fetch(at):
        if at > 0:
            sent = blocks[at - 1][-1]
            if at > 2:
                sent = after(sent, *work[at - 1]["other"])[0]
            blocks[at] = [pass_row(sent)]
        while len(blocks[at]) < group:
            blocks[at].append(pass_row(blocks[at][-1]))

    def mirror(at):
        w = work[at]
        if at == 1:
            blocks[at][-1], *work[0]["h_came"] = after(blocks[at][-1], *work[0]["h_came"])
        elif at > 1:
            blocks[at][-1] = after(blocks[at][-1])
        w["mine"] = blocks[at][0] if group == 1 else jnp.concatenate(blocks[at])
        eighth = w["mine"].shape[0] // (2 * n_col)
        bounds = [0, *((), (3, 6), (4,), (4,))[at], 2 * n_col]
        w["other"] = [swap_dp(w["mine"][i * eighth : j * eighth]) for i, j in zip(bounds[:-1], bounds[1:])]

    def arrived(at):
        nonlocal token
        token = (*token, blocks[at][-1])

    def build_kernel(mine, *others):
        def body(mine_ref, *refs):
            pieces = [(ref, k) for ref in refs[:-2] for k in range(ref.shape[0] // quarter)]
            for part, out in enumerate(refs[-2:]):
                for i in range(n_col):
                    ref, k = pieces[part * n_col + i]
                    out[pl.ds(2 * i * quarter, quarter), :] = mine_ref[pl.ds(part * rows + i * quarter, quarter), :]
                    out[pl.ds((2 * i + 1) * quarter, quarter), :] = ref[pl.ds(k * quarter, quarter), :]

        return call(
            body, [mine, *others], [whole] * (1 + len(others)), [shape((2 * rows, width), b16)] * 2, [whole] * 2, (), "build"
        )

    def build(at):
        nonlocal token
        w = work[at]
        mine, *others = after(w["mine"], *w["other"])
        if aligned:
            w["in"], w["cot"] = build_kernel(mine, *others)
        else:
            other = jnp.concatenate(others)
            pair = [a.reshape(group, 2 * n_col, quarter, width).transpose(1, 0, 2, 3) for a in (mine, other)]
            w["in"], w["cot"] = jnp.stack(pair, axis=2).reshape(2, 2 * tall, width)
        token = (w["in"], w["cot"])

    hidden_of = up_weight.shape[1]
    cuts = [cut_of(hidden_of), hidden_of, hidden_of, hidden_of]

    def products(at):
        nonlocal token
        w = work[at]
        w["h"], *w["h_out"] = token = first_product(after(w["in"]), up_weight, 0, cuts[at], "hidden_product")
        w["g"], *w["g_out"] = token = first_product(after(w["cot"]), down_weight, 1, cuts[at], "delta_act_product")

    def reduce_first(at):
        w = work[at]
        if at == 0:
            w["h_came"] = [swap_x(w["h_out"][0]), swap_y(w["h_out"][1])]
            w["g_came"] = [swap_y(w["g_out"][0]), swap_x(w["g_out"][1])]
            return
        h_out, g_out = w["h_out"][0], w["g_out"][0]
        if at > 1:
            h_out, g_out = after(h_out, g_out)
        w["h_came"], w["g_came"] = swap_x(h_out), swap_y(g_out)

    def reduce_second(at):
        nonlocal token
        w = work[at]
        if at == 0:
            h, h0, h1, g, g0, g1 = after(w["h"], *w["h_came"], w["g"], *w["g_came"])
            sent_h, w["h"], sent_g, w["g"] = token = add_crossed(h, (h0, h1), g, (g0, g1), cuts[0], FIRST_SUM)
        else:
            sent_h, w["h"], sent_g, w["g"] = token = add_halves(*after(w["h"], w["h_came"], w["g"], w["g_came"]), 1000)
        w["h_came"], w["g_came"] = swap_y(sent_h), swap_x(sent_g)

    def gather_first(at):
        nonlocal token
        w = work[at]
        w["active"], w["delta"] = token = activate(*after(w["h"], w["h_came"], w["g"], w["g_came"]), cuts[at])
        w["delta_came"], w["active_came"] = swap_y(w["delta"]), swap_x(w["active"])

    def join(at, flops=1000):
        nonlocal token
        w = work[at]
        w["delta"], w["active"] = token = join_pairs(
            flops, *after(w["delta"], w["delta_came"], w["active"], w["active_came"])
        )

    def gather_second(at):
        w = work[at]
        join(at, ODD_JOIN if at % 2 else 1000)
        w["delta_came"], w["active_came"] = swap_x(w["delta"]), swap_y(w["active"])

    def add_kernel(dtype, *arrays):
        tile = tile_of(width, 768)

        def body(*refs):
            refs[-1][...] = add_shares(*refs[:-1]).astype(dtype)

        blocks_of = [pl.BlockSpec((a.shape[0], tile), lambda i: (0, i)) for a in arrays]
        return call(body, arrays, blocks_of, shape((rows, width), dtype), blocks_of[0], (width // tile,), "add")

    def share(at):
        nonlocal token
        w = work[at]
        delta = after(w["delta"])
        if not aligned:
            parts = contract(delta, up_weight, 1, 1).reshape(n_col, group, 2, quarter, width)
            token = (parts,)
            w["part"], w["part_came"] = parts[:, :, 0], swap_dp(parts[:, :, 1])
        else:
            w["part"], *sent = token = input_product(delta, up_weight, quarter, 1 if at < 2 else 2)
            w["part_came"] = [swap_dp(part) for part in sent]

    running = None

    def share_sum(at):
        nonlocal token, running
        w = work[at]
        if not aligned:
            part = w["part"] + w["part_came"]
            for step in range(at * group, (at + 1) * group):
                one = part[:, step - at * group].reshape(rows, width)
                if step == 0:
                    w["part"] = one
                else:
                    running = pass_row(one if running is None else running + one)
        elif at == 1:
            running = pass_row(add_kernel(f32, w["part"], *w["part_came"]))
        else:
            total = add_kernel(b16 if at == 3 else f32, *after(w["part"], *w["part_came"], running))
            token = (total,)
            running = pass_row(total)

    def settle():
        nonlocal token
        token = (*token, running)

    def early(names, held, name):
        nonlocal token
        values = after(*(work[at][k] for k in names for at in (0, 1)))
        token = (early_grad(values[:2], values[2:], held, name),)
        return token[0]

    def late(names, partial, held, name):
        nonlocal token
        values = after(*(work[at][k] for k in names for at in (2, 3)))
        token = (late_grad(values[:2], values[2:], partial, held, 1.0 / replicas, name),)
        return token[0]

    fetch(0)
    mirror(0)
    fetch(1)
    build(0)
    products(0)
    reduce_first(0)
    mirror(1)
    build(1)
    products(1)
    reduce_first(1)
    reduce_second(0)
    fetch(2)
    reduce_second(1)
    gather_first(0)
    gather_first(1)
    arrived(2)
    mirror(2)
    gather_second(0)
    build(2)
    products(2)
    fetch(3)
    gather_second(1)
    join(0)
    reduce_first(2)
    arrived(3)
    mirror(3)
    build(3)
    products(3)
    share(0)
    if not aligned:
        share_sum(0)
    join(1)
    reduce_first(3)
    share(1)
    share_sum(1)
    up_partial = early(("in", "delta"), True, "up_grad_early")
    reduce_second(2)
    reduce_second(3)
    gather_first(2)
    gather_first(3)
    gather_second(2)
    down_partial = early(("active", "cot"), False, "down_grad_early")
    settle()
    gather_second(3)
    join(2)
    share(2)
    share_sum(2)
    join(3)
    share(3)
    up_grad = late(("in", "delta"), up_partial, True, "up_grad")
    share_sum(3)
    down_grad = late(("active", "cot"), down_partial, False, "down_grad")

    def end_kernel(*arrays):
        tile = tile_of(width, 768)

        def body(own_ref, *refs):
            total = add_shares(*refs[:-1]).astype(b16)
            for i in range(n_col):
                target = pl.multiple_of((own_ref[0] ^ x_outer[i]) * quarter, quarter)
                refs[-1][pl.ds(target, quarter), :] = total[i * quarter : (i + 1) * quarter]

        blocks_of = [pl.BlockSpec((a.shape[0], tile), lambda i: (0, i)) for a in arrays]
        return call(
            body,
            [own.astype(jnp.int32).reshape(1), *arrays],
            [pl.BlockSpec(memory_space=pltpu.SMEM)] + blocks_of,
            shape((rows, width), b16),
            blocks_of[0],
            (width // tile,),
            "end",
        )

    if aligned:
        return (end_kernel(work[0]["part"], *work[0]["part_came"], running), up_grad, down_grad)
    input_grad = work[0]["part"] + running.astype(f32)
    input_grad = input_grad.astype(b16).reshape(2, 2, quarter, width).transpose(1, 0, 2, 3).reshape(rows, width)
    return (reorder(input_grad, y_outer), up_grad, down_grad)


def solution(mesh):
    tokens = P(("dp", "row"), "col")
    up, down = P("col", ("dp", "row")), P(("dp", "row"), "col")
    return jax.shard_map(
        shards,
        mesh=mesh,
        in_specs=(tokens, up, down, tokens),
        out_specs=(tokens, up, down),
        check_vma=False,
    )
```

profile of v0, /device:TPU:0, one launch (start us, length us, event | category | flops | bytes accessed | tf_op | source)
XLA Modules:
  0.0 254.7 jit_solution(7443622912061702072)
XLA Ops:
  2.4 2.6 %collective-permute-start.1 = (bf16[256,1536]{1,0:T(8,128)(2,1)S(1)}, bf16[256,1536]{1,0:T(8,128)(2,1)S(1)}, u32[]{:S(2)}, u32[]{:S(2)}) collective-permute-start(bf16[256,1536]{1,0:T(8,128)(2,1)S(1)} %reorder.1.mine_ref), channel_id=1, source_target_pairs={{0,4},{4,8},{8,12},{12,0},{1,5},{5,9},{9,13},{13,1},{2,6},{6,10},{... | collective-permute-start | bytes 2359304 | tf_op jit(solution)/shard_map/ppermute | solution.py:293
  5.2 3.7 %copy-done = bf16[1536,3072]{1,0:T(8,128)(2,1)S(1)} copy-done((bf16[1536,3072]{1,0:T(8,128)(2,1)S(1)}, bf16[1536,3072]{1,0:T(8,128)(2,1)}, u32[]{:S(2)}) %copy-start) | copy-done | bytes 9437208
  8.9 2.6 %hidden_product.4 = (f32[128,3072]{1,0:T(8,128)S(1)}, bf16[128,1536]{1,0:T(8,128)(2,1)S(1)}, bf16[128,1536]{1,0:T(8,128)(2,1)S(1)}) custom-call(bf16[256,1536]{1,0:T(8,128)(2,1)S(1)} %get-tuple-element.319.chunk_ref.refs_0_, bf16[1536,3072]{1,0:T(8,128)(2,1)S(1)} %copy-done), custom_call_target="tpu_custom_call" | custom-call | flops 1000 | bytes 1000 | tf_op jit(solution)/shard_map/hidden_product/pallas_call | solution.py:30
  11.5 2.2 collective-permute-start.2
  15.2 3.7 %copy-done.1 = bf16[3072,1536]{1,0:T(8,128)(2,1)S(1)} copy-done((bf16[3072,1536]{1,0:T(8,128)(2,1)S(1)}, bf16[3072,1536]{1,0:T(8,128)(2,1)}, u32[]{:S(2)}) %copy-start.1) | copy-done | bytes 9437208
  18.9 2.6 %delta_act_product.4 = (f32[128,3072]{1,0:T(8,128)S(1)}, bf16[128,1536]{1,0:T(8,128)(2,1)S(1)}, bf16[128,1536]{1,0:T(8,128)(2,1)S(1)}) custom-call(bf16[256,1536]{1,0:T(8,128)(2,1)S(1)} %get-tuple-element.359.chunk_ref.refs_2_, bf16[3072,1536]{1,0:T(8,128)(2,1)S(1)} %copy-done.1), custom_call_target="tpu_custom_call" | custom-call | flops 1000 | bytes 1000 | tf_op jit(solution)/shard_map/delta_act_product/pallas_call | solution.py:30
  22.2 3.1 %collective-permute-done.1.mine_ref = bf16[256,1536]{1,0:T(8,128)(2,1)S(1)} collective-permute-done((bf16[256,1536]{1,0:T(8,128)(2,1)S(1)}, bf16[256,1536]{1,0:T(8,128)(2,1)S(1)}, u32[]{:S(2)}, u32[]{:S(2)}) %collective-permute-start.1) | collective-permute-done | bytes 786464 | tf_op jit(solution)/shard_map/ppermute | solution.py:293
  29.6 2.6 %hidden_product.5 = (f32[128,3072]{1,0:T(8,128)S(1)}, bf16[128,3072]{1,0:T(8,128)(2,1)S(1)}) custom-call(bf16[256,1536]{1,0:T(8,128)(2,1)S(1)} %get-tuple-element.320.chunk_ref.refs_1_, bf16[1536,3072]{1,0:T(8,128)(2,1)S(1)} %bitcast.2), custom_call_target="tpu_custom_call" | custom-call | flops 1000 | bytes 1000 | tf_op jit(solution)/shard_map/hidden_product/pallas_call | solution.py:30
  32.8 2.6 %delta_act_product.5 = (f32[128,3072]{1,0:T(8,128)S(1)}, bf16[128,3072]{1,0:T(8,128)(2,1)S(1)}) custom-call(bf16[256,1536]{1,0:T(8,128)(2,1)S(1)} %get-tuple-element.360.chunk_ref.refs_3_, bf16[3072,1536]{1,0:T(8,128)(2,1)S(1)} %bitcast.4), custom_call_target="tpu_custom_call" | custom-call | flops 1000 | bytes 1000 | tf_op jit(solution)/shard_map/delta_act_product/pallas_call | solution.py:30
  35.4 2.0 collective-permute-start.12
  39.3 13.3 %collective-permute-done.11.ch = bf16[128,3072]{1,0:T(8,128)(2,1)S(1)} collective-permute-done((bf16[128,3072]{1,0:T(8,128)(2,1)S(1)}, bf16[128,3072]{1,0:T(8,128)(2,1)S(1)}, u32[]{:S(2)}, u32[]{:S(2)}) %collective-permute-start.11) | collective-permute-done | bytes 786464 | tf_op jit(solution)/shard_map/ppermute | solution.py:284
  52.7 3.3 %collective-permute-done.12.cg = bf16[128,3072]{1,0:T(8,128)(2,1)S(1)} collective-permute-done((bf16[128,3072]{1,0:T(8,128)(2,1)S(1)}, bf16[128,3072]{1,0:T(8,128)(2,1)S(1)}, u32[]{:S(2)}, u32[]{:S(2)}) %collective-permute-start.12) | collective-permute-done | bytes 786464 | tf_op jit(solution)/shard_map/ppermute | solution.py:287
  56.8 2.0 collective-permute-start.15
  60.3 4.1 %collective-permute-done.9.ch = bf16[64,3072]{1,0:T(8,128)(2,1)S(1)} collective-permute-done((bf16[64,3072]{1,0:T(8,128)(2,1)S(1)}, bf16[64,3072]{1,0:T(8,128)(2,1)S(1)}, u32[]{:S(2)}, u32[]{:S(2)}) %collective-permute-start.9) | collective-permute-done | bytes 393248 | tf_op jit(solution)/shard_map/ppermute | solution.py:287
  65.4 2.0 collective-permute-start.13
  68.9 3.9 %collective-permute-done.15.ch = bf16[64,3072]{1,0:T(8,128)(2,1)S(1)} collective-permute-done((bf16[64,3072]{1,0:T(8,128)(2,1)S(1)}, bf16[64,3072]{1,0:T(8,128)(2,1)S(1)}, u32[]{:S(2)}, u32[]{:S(2)}) %collective-permute-start.15) | collective-permute-done | bytes 393248 | tf_op jit(solution)/shard_map/ppermute | solution.py:287
  75.9 4.1 %collective-permute-done.13.refs_1_ = bf16[64,3072]{1,0:T(8,128)(2,1)S(1)} collective-permute-done((bf16[64,3072]{1,0:T(8,128)(2,1)S(1)}, bf16[64,3072]{1,0:T(8,128)(2,1)S(1)}, u32[]{:S(2)}, u32[]{:S(2)}) %collective-permute-start.13) | collective-permute-done | bytes 393248 | tf_op jit(solution)/shard_map/ppermute | solution.py:287
  84.1 3.5 %hidden_product.6 = (f32[128,3072]{1,0:T(8,128)S(1)}, bf16[128,3072]{1,0:T(8,128)(2,1)}) custom-call(bf16[256,1536]{1,0:T(8,128)(2,1)S(1)} %get-tuple-element.391.chunk_ref.refs_0_, bf16[1536,3072]{1,0:T(8,128)(2,1)S(1)} %bitcast.2), custom_call_target="tpu_custom_call" | custom-call | flops 1000 | bytes 1000 | tf_op jit(solution)/shard_map/hidden_product/pallas_call | solution.py:30
  87.6 3.5 %delta_act_product.6 = (f32[128,3072]{1,0:T(8,128)S(1)}, bf16[128,3072]{1,0:T(8,128)(2,1)}) custom-call(bf16[256,1536]{1,0:T(8,128)(2,1)S(1)} %get-tuple-element.401.chunk_ref.refs_2_, bf16[3072,1536]{1,0:T(8,128)(2,1)S(1)} %bitcast.4), custom_call_target="tpu_custom_call" | custom-call | flops 1000 | bytes 1000 | tf_op jit(solution)/shard_map/delta_act_product/pallas_call | solution.py:30
  92.0 1.8 collective-permute-start.24
  97.5 5.7 %collective-permute-done.18.refs_1_ = bf16[128,3072]{1,0:T(8,128)(2,1)S(1)} collective-permute-done((bf16[128,3072]{1,0:T(8,128)(2,1)S(1)}, bf16[128,3072]{1,0:T(8,128)(2,1)S(1)}, u32[]{:S(2)}, u32[]{:S(2)}) %collective-permute-start.18) | collective-permute-done | bytes 786464 | tf_op jit(solution)/shard_map/ppermute | solution.py:284
  103.2 5.7 %collective-permute-done.19.refs_3_ = bf16[128,3072]{1,0:T(8,128)(2,1)S(1)} collective-permute-done((bf16[128,3072]{1,0:T(8,128)(2,1)S(1)}, bf16[128,3072]{1,0:T(8,128)(2,1)S(1)}, u32[]{:S(2)}, u32[]{:S(2)}) %collective-permute-start.19) | collective-permute-done | bytes 786464 | tf_op jit(solution)/shard_map/ppermute | solution.py:287
  114.2 3.5 %hidden_product.7 = (f32[128,3072]{1,0:T(8,128)S(1)}, bf16[128,3072]{1,0:T(8,128)(2,1)}) custom-call(bf16[256,1536]{1,0:T(8,128)(2,1)S(1)} %get-tuple-element.392.chunk_ref.refs_1_, bf16[1536,3072]{1,0:T(8,128)(2,1)S(1)} %bitcast.2), custom_call_target="tpu_custom_call" | custom-call | flops 1000 | bytes 1000 | tf_op jit(solution)/shard_map/hidden_product/pallas_call | solution.py:30
  117.7 3.5 %delta_act_product.7 = (f32[128,3072]{1,0:T(8,128)S(1)}, bf16[128,3072]{1,0:T(8,128)(2,1)}) custom-call(bf16[256,1536]{1,0:T(8,128)(2,1)S(1)} %get-tuple-element.402.chunk_ref.refs_3_, bf16[3072,1536]{1,0:T(8,128)(2,1)S(1)} %bitcast.4), custom_call_target="tpu_custom_call" | custom-call | flops 1000 | bytes 1000 | tf_op jit(solution)/shard_map/delta_act_product/pallas_call | solution.py:30
  121.2 3.5 %input_product.4 = (f32[128,1536]{1,0:T(8,128)S(1)}, f32[128,1536]{1,0:T(8,128)}) custom-call(bf16[256,3072]{1,0:T(8,128)(2,1)S(1)} %get-tuple-element.321.delta_ref.refs_2_, bf16[1536,3072]{1,0:T(8,128)(2,1)S(1)} %bitcast.2), custom_call_target="tpu_custom_call" | custom-call | flops 1000 | bytes 1000 | tf_op jit(solution)/shard_map/input_product/pallas_call | solution.py:30
  129.7 2.6 %input_product.5 = (f32[128,1536]{1,0:T(8,128)S(1)}, f32[128,1536]{1,0:T(8,128)S(1)}) custom-call(bf16[256,3072]{1,0:T(8,128)(2,1)S(1)} %get-tuple-element.322.delta_ref.refs_3_, bf16[1536,3072]{1,0:T(8,128)(2,1)S(1)} %bitcast.2), custom_call_target="tpu_custom_call" | custom-call | flops 1000 | bytes 1000 | tf_op jit(solution)/shard_map/input_product/pallas_call | solution.py:30
  132.5 6.1 %up_grad_early.1.refs_4_ = f32[1536,3072]{1,0:T(8,128)S(1)} custom-call(bf16[256,1536]{1,0:T(8,128)(2,1)S(1)} %get-tuple-element.319.chunk_ref.refs_0_, bf16[256,1536]{1,0:T(8,128)(2,1)S(1)} %get-tuple-element.320.chunk_ref.refs_1_, bf16[256,3072]{1,0:T(8,128)(2,1)S(1)} %get-tuple-element.321.delta_ref.refs_2_, ...), custom_call_target="tpu_custom_call" | custom-call | flops 1000 | bytes 1000 | tf_op jit(solution)/shard_map/up_grad_early/pallas_call | solution.py:30
  138.6 4.0 %collective-permute-done.33.cg = bf16[128,3072]{1,0:T(8,128)(2,1)S(1)} collective-permute-done((bf16[128,3072]{1,0:T(8,128)(2,1)}, bf16[128,3072]{1,0:T(8,128)(2,1)S(1)}, u32[]{:S(2)}, u32[]{:S(2)}) %collective-permute-start.33) | collective-permute-done | bytes 786464 | tf_op jit(solution)/shard_map/ppermute | solution.py:287
  145.5 1.8 collective-permute-start.36
  148.8 5.0 %collective-permute-done.30.ch = bf16[128,3072]{1,0:T(8,128)(2,1)S(1)} collective-permute-done((bf16[128,3072]{1,0:T(8,128)(2,1)}, bf16[128,3072]{1,0:T(8,128)(2,1)S(1)}, u32[]{:S(2)}, u32[]{:S(2)}) %collective-permute-start.30) | collective-permute-done | bytes 786464 | tf_op jit(solution)/shard_map/ppermute | solution.py:284
  153.8 5.7 %collective-permute-done.31.cg = bf16[128,3072]{1,0:T(8,128)(2,1)S(1)} collective-permute-done((bf16[128,3072]{1,0:T(8,128)(2,1)}, bf16[128,3072]{1,0:T(8,128)(2,1)S(1)}, u32[]{:S(2)}, u32[]{:S(2)}) %collective-permute-start.31) | collective-permute-done | bytes 786464 | tf_op jit(solution)/shard_map/ppermute | solution.py:287
  160.3 1.8 collective-permute-start.34
  163.9 1.9 collective-permute-start.43
  165.8 2.1 collective-permute-done.36.ch
  172.1 4.2 %collective-permute-done.34.ch = bf16[64,3072]{1,0:T(8,128)(2,1)S(1)} collective-permute-done((bf16[64,3072]{1,0:T(8,128)(2,1)S(1)}, bf16[64,3072]{1,0:T(8,128)(2,1)S(1)}, u32[]{:S(2)}, u32[]{:S(2)}) %collective-permute-start.34) | collective-permute-done | bytes 393248 | tf_op jit(solution)/shard_map/ppermute | solution.py:287
  177.2 1.8 collective-permute-start.38
  180.6 4.2 %collective-permute-done.40.refs_1_ = bf16[64,3072]{1,0:T(8,128)(2,1)S(1)} collective-permute-done((bf16[64,3072]{1,0:T(8,128)(2,1)S(1)}, bf16[64,3072]{1,0:T(8,128)(2,1)S(1)}, u32[]{:S(2)}, u32[]{:S(2)}) %collective-permute-start.40) | collective-permute-done | bytes 393248 | tf_op jit(solution)/shard_map/ppermute | solution.py:287
  188.4 9.1 %down_grad_early.1.refs_4_ = f32[3072,1536]{1,0:T(8,128)} custom-call(bf16[256,3072]{1,0:T(8,128)(2,1)S(1)} %get-tuple-element.357.refs_0_, bf16[256,3072]{1,0:T(8,128)(2,1)S(1)} %get-tuple-element.358.refs_1_, bf16[256,1536]{1,0:T(8,128)(2,1)S(1)} %get-tuple-element.359.chunk_ref.refs_2_, bf16[256,1536]{1,0:T(8,128)(2,1)S(1)} %get-tuple-element.360.chunk_ref.refs_3_), custom_call_target="tpu_custom_call" | custom-call | flops 1000 | bytes 1000 | tf_op jit(solution)/shard_map/down_grad_early/pallas_call | solution.py:30
  198.8 8.2 %collective-permute-done.46.refs_1_ = bf16[128,3072]{1,0:T(8,128)(2,1)S(1)} collective-permute-done((bf16[128,3072]{1,0:T(8,128)(2,1)S(1)}, bf16[128,3072]{1,0:T(8,128)(2,1)S(1)}, u32[]{:S(2)}, u32[]{:S(2)}) %collective-permute-start.46) | collective-permute-done | bytes 786464 | tf_op jit(solution)/shard_map/ppermute | solution.py:284
  207.0 3.0 %collective-permute-done.47.refs_3_ = bf16[128,3072]{1,0:T(8,128)(2,1)S(1)} collective-permute-done((bf16[128,3072]{1,0:T(8,128)(2,1)S(1)}, bf16[128,3072]{1,0:T(8,128)(2,1)S(1)}, u32[]{:S(2)}, u32[]{:S(2)}) %collective-permute-start.47) | collective-permute-done | bytes 786464 | tf_op jit(solution)/shard_map/ppermute | solution.py:287
  210.7 2.6 %input_product.6 = (f32[128,1536]{1,0:T(8,128)S(1)}, f32[64,1536]{1,0:T(8,128)S(1)}, f32[64,1536]{1,0:T(8,128)S(1)}) custom-call(bf16[256,3072]{1,0:T(8,128)(2,1)S(1)} %get-tuple-element.393.delta_ref.refs_2_, bf16[1536,3072]{1,0:T(8,128)(2,1)S(1)} %bitcast.2), custom_call_target="tpu_custom_call" | custom-call | flops 1000 | bytes 1000 | tf_op jit(solution)/shard_map/input_product/pallas_call | solution.py:30
  218.5 2.1 collective-permute-done.44.refs_1_
  220.5 4.2 %collective-permute-done.45.refs_3_ = bf16[128,3072]{1,0:T(8,128)(2,1)S(1)} collective-permute-done((bf16[128,3072]{1,0:T(8,128)(2,1)S(1)}, bf16[128,3072]{1,0:T(8,128)(2,1)S(1)}, u32[]{:S(2)}, u32[]{:S(2)}) %collective-permute-start.45) | collective-permute-done | bytes 786464 | tf_op jit(solution)/shard_map/ppermute | solution.py:287
  225.4 3.3 %input_product.7 = (f32[128,1536]{1,0:T(8,128)S(1)}, f32[64,1536]{1,0:T(8,128)}, f32[64,1536]{1,0:T(8,128)S(1)}) custom-call(bf16[256,3072]{1,0:T(8,128)(2,1)S(1)} %get-tuple-element.394.delta_ref.refs_3_, bf16[1536,3072]{1,0:T(8,128)(2,1)S(1)} %bitcast.2), custom_call_target="tpu_custom_call" | custom-call | flops 1000 | bytes 1000 | tf_op jit(solution)/shard_map/input_product/pallas_call | solution.py:30
  230.2 7.6 %up_grad.1 = bf16[1536,3072]{1,0:T(8,128)(2,1)} custom-call(bf16[256,1536]{1,0:T(8,128)(2,1)S(1)} %get-tuple-element.391.chunk_ref.refs_0_, bf16[256,1536]{1,0:T(8,128)(2,1)S(1)} %copy-done.3, bf16[256,3072]{1,0:T(8,128)(2,1)S(1)} %get-tuple-element.393.delta_ref.refs_2_, bf16[256,3072]{1,0:T(8,128)(2,1)S(1)} %get-tuple-element.394.delta_ref.refs_3_, ...), custom_call_target="tpu_custom_call" | custom-call | flops 1000 | bytes 1000 | tf_op jit(solution)/shard_map/up_grad/pallas_call | solution.py:30
  238.6 2.1 add.5
  241.6 7.5 %down_grad.1 = bf16[3072,1536]{1,0:T(8,128)(2,1)} custom-call(bf16[256,3072]{1,0:T(8,128)(2,1)S(1)} %copy-done.5, bf16[256,3072]{1,0:T(8,128)(2,1)S(1)} %copy-done.7, bf16[256,1536]{1,0:T(8,128)(2,1)S(1)} %get-tuple-element.401.chunk_ref.refs_2_, bf16[256,1536]{1,0:T(8,128)(2,1)S(1)} %get-tuple-element.402.chunk_ref.refs_3_, f32[3072,1536]{1,0:T(8,128)S(1)} %bitcast.6), custom_call_target="tpu_custom_call" | custom-call | flops 1000 | bytes 1000 | tf_op jit(solution)/shard_map/down_grad/pallas_call | solution.py:30
  249.1 4.1 %collective-permute-done.53.refs_2_ = bf16[128,1536]{1,0:T(8,128)(2,1)S(1)} collective-permute-done((bf16[128,1536]{1,0:T(8,128)(2,1)S(1)}, bf16[128,1536]{1,0:T(8,128)(2,1)S(1)}, u32[]{:S(2)}, u32[]{:S(2)}) %collective-permute-start.53) | collective-permute-done | bytes 393248 | tf_op jit(solution)/shard_map/ppermute | solution.py:293
  (174 shorter events, 67.0 us)
Async XLA Ops:
  2.4 22.8 %collective-permute-start.1 = (bf16[256,1536]{1,0:T(8,128)(2,1)S(1)}, bf16[256,1536]{1,0:T(8,128)(2,1)S(1)}, u32[]{:S(2)}, u32[]{:S(2)}) collective-permute-start(bf16[256,1536]{1,0:T(8,128)(2,1)S(1)} %reorder.1.mine_ref), channel_id=1, source_target_pairs={{0,4},{4,8},{8,12},{12,0},{1,5},{5,9},{9,13},{13,1},{2,6},{6,10},{... | collective-permute-start | bytes 2359304 | tf_op jit(solution)/shard_map/ppermute | solution.py:293
  11.5 13.8 %collective-permute-start.2 = (bf16[128,1536]{1,0:T(8,128)(2,1)S(1)}, bf16[128,1536]{1,0:T(8,128)(2,1)S(1)}, u32[]{:S(2)}, u32[]{:S(2)}) collective-permute-start(bf16[128,1536]{1,0:T(8,128)(2,1)S(1)} %get-tuple-element.209), channel_id=1, source_target_pairs={{0,1},{1,0},{2,3},{3,2},{4,5},{5,4},{6,7},{7,6},{8,9},{9,8},{10,11... | collective-permute-start | bytes 1179656 | tf_op jit(solution)/shard_map/ppermute | solution.py:284
  13.7 11.6 %collective-permute-start.3 = (bf16[128,1536]{1,0:T(8,128)(2,1)S(1)}, bf16[128,1536]{1,0:T(8,128)(2,1)S(1)}, u32[]{:S(2)}, u32[]{:S(2)}) collective-permute-start(bf16[128,1536]{1,0:T(8,128)(2,1)S(1)} %get-tuple-element.210), channel_id=1, source_target_pairs={{0,2},{1,3},{2,0},{3,1},{4,6},{5,7},{6,4},{7,5},{8,10},{9,11},{10,... | collective-permute-start | bytes 1179656 | tf_op jit(solution)/shard_map/ppermute | solution.py:287
  21.5 15.9 %collective-permute-start.4 = (bf16[128,1536]{1,0:T(8,128)(2,1)S(1)}, bf16[128,1536]{1,0:T(8,128)(2,1)S(1)}, u32[]{:S(2)}, u32[]{:S(2)}) collective-permute-start(bf16[128,1536]{1,0:T(8,128)(2,1)S(1)} %get-tuple-element.213), channel_id=1, source_target_pairs={{0,2},{1,3},{2,0},{3,1},{4,6},{5,7},{6,4},{7,5},{8,10},{9,11},{10,... | collective-permute-start | bytes 1179656 | tf_op jit(solution)/shard_map/ppermute | solution.py:287
  22.1 15.3 %collective-permute-start.5 = (bf16[128,1536]{1,0:T(8,128)(2,1)S(1)}, bf16[128,1536]{1,0:T(8,128)(2,1)S(1)}, u32[]{:S(2)}, u32[]{:S(2)}) collective-permute-start(bf16[128,1536]{1,0:T(8,128)(2,1)S(1)} %get-tuple-element.214), channel_id=1, source_target_pairs={{0,1},{1,0},{2,3},{3,2},{4,5},{5,4},{6,7},{7,6},{8,9},{9,8},{10,11... | collective-permute-start | bytes 1179656 | tf_op jit(solution)/shard_map/ppermute | solution.py:284
  25.3 4.1 %collective-permute-start.7 = (bf16[96,1536]{1,0:T(8,128)(2,1)S(1)}, bf16[96,1536]{1,0:T(8,128)(2,1)S(1)}, u32[]{:S(2)}, u32[]{:S(2)}) collective-permute-start(bf16[96,1536]{1,0:T(8,128)(2,1)S(1)} %get-tuple-element.407), channel_id=1, source_target_pairs={{0,16},{16,0},{1,17},{17,1},{2,18},{18,2},{3,19},{19,3},{4,20},{20... | collective-permute-start | bytes 884744 | tf_op jit(solution)/shard_map/ppermute | solution.py:290
  25.4 4.0 %collective-permute-start.6 = (bf16[96,1536]{1,0:T(8,128)(2,1)S(1)}, bf16[96,1536]{1,0:T(8,128)(2,1)S(1)}, u32[]{:S(2)}, u32[]{:S(2)}) collective-permute-start(bf16[96,1536]{1,0:T(8,128)(2,1)S(1)} %get-tuple-element.408), channel_id=1, source_target_pairs={{0,16},{16,0},{1,17},{17,1},{2,18},{18,2},{3,19},{19,3},{4,20},{20... | collective-permute-start | bytes 884744 | tf_op jit(solution)/shard_map/ppermute | solution.py:290
  27.7 46.1 %collective-permute-start.17 = (bf16[256,1536]{1,0:T(8,128)(2,1)S(1)}, bf16[256,1536]{1,0:T(8,128)(2,1)S(1)}, u32[]{:S(2)}, u32[]{:S(2)}) collective-permute-start(bf16[256,1536]{1,0:T(8,128)(2,1)S(1)} %collective-permute-done.1.mine_ref), channel_id=1, source_target_pairs={{0,4},{4,8},{8,12},{12,0},{1,5},{5,9},{9,13},{13,1},{2,6},{6,10},{... | collective-permute-start | bytes 2359304 | tf_op jit(solution)/shard_map/ppermute | solution.py:293
  32.2 20.5 %collective-permute-start.11 = (bf16[128,3072]{1,0:T(8,128)(2,1)S(1)}, bf16[128,3072]{1,0:T(8,128)(2,1)S(1)}, u32[]{:S(2)}, u32[]{:S(2)}) collective-permute-start(bf16[128,3072]{1,0:T(8,128)(2,1)S(1)} %get-tuple-element.226), channel_id=1, source_target_pairs={{0,1},{1,0},{2,3},{3,2},{4,5},{5,4},{6,7},{7,6},{8,9},{9,8},{10,11... | collective-permute-start | bytes 2359304 | tf_op jit(solution)/shard_map/ppermute | solution.py:284
  35.4 20.5 %collective-permute-start.12 = (bf16[128,3072]{1,0:T(8,128)(2,1)S(1)}, bf16[128,3072]{1,0:T(8,128)(2,1)S(1)}, u32[]{:S(2)}, u32[]{:S(2)}) collective-permute-start(bf16[128,3072]{1,0:T(8,128)(2,1)S(1)} %get-tuple-element.229), channel_id=1, source_target_pairs={{0,2},{1,3},{2,0},{3,1},{4,6},{5,7},{6,4},{7,5},{8,10},{9,11},{10,... | collective-permute-start | bytes 2359304 | tf_op jit(solution)/shard_map/ppermute | solution.py:287
  37.7 26.7 %collective-permute-start.9 = (bf16[64,3072]{1,0:T(8,128)(2,1)S(1)}, bf16[64,3072]{1,0:T(8,128)(2,1)S(1)}, u32[]{:S(2)}, u32[]{:S(2)}) collective-permute-start(bf16[64,3072]{1,0:T(8,128)(2,1)S(1)} %get-tuple-element.237), channel_id=1, source_target_pairs={{0,2},{1,3},{2,0},{3,1},{4,6},{5,7},{6,4},{7,5},{8,10},{9,11},{10,... | collective-permute-start | bytes 1179656 | tf_op jit(solution)/shard_map/ppermute | solution.py:287
  37.8 26.5 %collective-permute-start.10 = (bf16[64,3072]{1,0:T(8,128)(2,1)S(1)}, bf16[64,3072]{1,0:T(8,128)(2,1)S(1)}, u32[]{:S(2)}, u32[]{:S(2)}) collective-permute-start(bf16[64,3072]{1,0:T(8,128)(2,1)S(1)} %get-tuple-element.239), channel_id=1, source_target_pairs={{0,1},{1,0},{2,3},{3,2},{4,5},{5,4},{6,7},{7,6},{8,9},{9,8},{10,11... | collective-permute-start | bytes 1179656 | tf_op jit(solution)/shard_map/ppermute | solution.py:284
  56.8 16.0 %collective-permute-start.15 = (bf16[64,3072]{1,0:T(8,128)(2,1)S(1)}, bf16[64,3072]{1,0:T(8,128)(2,1)S(1)}, u32[]{:S(2)}, u32[]{:S(2)}) collective-permute-start(bf16[64,3072]{1,0:T(8,128)(2,1)S(1)} %get-tuple-element.244), channel_id=1, source_target_pairs={{0,2},{1,3},{2,0},{3,1},{4,6},{5,7},{6,4},{7,5},{8,10},{9,11},{10,... | collective-permute-start | bytes 1179656 | tf_op jit(solution)/shard_map/ppermute | solution.py:287
  58.8 14.0 %collective-permute-start.16 = (bf16[64,3072]{1,0:T(8,128)(2,1)S(1)}, bf16[64,3072]{1,0:T(8,128)(2,1)S(1)}, u32[]{:S(2)}, u32[]{:S(2)}) collective-permute-start(bf16[64,3072]{1,0:T(8,128)(2,1)S(1)} %get-tuple-element.246), channel_id=1, source_target_pairs={{0,1},{1,0},{2,3},{3,2},{4,5},{5,4},{6,7},{7,6},{8,9},{9,8},{10,11... | collective-permute-start | bytes 1179656 | tf_op jit(solution)/shard_map/ppermute | solution.py:284
  65.4 14.5 %collective-permute-start.13 = (bf16[64,3072]{1,0:T(8,128)(2,1)S(1)}, bf16[64,3072]{1,0:T(8,128)(2,1)S(1)}, u32[]{:S(2)}, u32[]{:S(2)}) collective-permute-start(bf16[64,3072]{1,0:T(8,128)(2,1)S(1)} %get-tuple-element.260.refs_0_), channel_id=1, source_target_pairs={{0,2},{1,3},{2,0},{3,1},{4,6},{5,7},{6,4},{7,5},{8,10},{9,11},{10,... | collective-permute-start | bytes 1179656 | tf_op jit(solution)/shard_map/ppermute | solution.py:287
  67.4 14.3 %collective-permute-start.14 = (bf16[64,3072]{1,0:T(8,128)(2,1)S(1)}, bf16[64,3072]{1,0:T(8,128)(2,1)S(1)}, u32[]{:S(2)}, u32[]{:S(2)}) collective-permute-start(bf16[64,3072]{1,0:T(8,128)(2,1)S(1)} %get-tuple-element.262.refs_2_), channel_id=1, source_target_pairs={{0,1},{1,0},{2,3},{3,2},{4,5},{5,4},{6,7},{7,6},{8,9},{9,8},{10,11... | collective-permute-start | bytes 1179656 | tf_op jit(solution)/shard_map/ppermute | solution.py:284
  73.8 9.9 %collective-permute-start.23 = (bf16[128,1536]{1,0:T(8,128)(2,1)S(1)}, bf16[128,1536]{1,0:T(8,128)(2,1)S(1)}, u32[]{:S(2)}, u32[]{:S(2)}) collective-permute-start(bf16[128,1536]{1,0:T(8,128)(2,1)S(1)} %get-tuple-element.405), channel_id=1, source_target_pairs={{0,16},{16,0},{1,17},{17,1},{2,18},{18,2},{3,19},{19,3},{4,20},{20... | collective-permute-start | bytes 1179656 | tf_op jit(solution)/shard_map/ppermute | solution.py:290
  73.9 10.1 %collective-permute-start.22 = (bf16[128,1536]{1,0:T(8,128)(2,1)S(1)}, bf16[128,1536]{1,0:T(8,128)(2,1)S(1)}, u32[]{:S(2)}, u32[]{:S(2)}) collective-permute-start(bf16[128,1536]{1,0:T(8,128)(2,1)S(1)} %get-tuple-element.406), channel_id=1, source_target_pairs={{0,16},{16,0},{1,17},{17,1},{2,18},{18,2},{3,19},{19,3},{4,20},{20... | collective-permute-start | bytes 1179656 | tf_op jit(solution)/shard_map/ppermute | solution.py:290
  74.4 16.7 %collective-permute-start.21 = (bf16[64,3072]{1,0:T(8,128)(2,1)S(1)}, bf16[64,3072]{1,0:T(8,128)(2,1)S(1)}, u32[]{:S(2)}, u32[]{:S(2)}) collective-permute-start(bf16[64,3072]{1,0:T(8,128)(2,1)S(1)} %get-tuple-element.280.refs_2_), channel_id=1, source_target_pairs={{0,1},{1,0},{2,3},{3,2},{4,5},{5,4},{6,7},{7,6},{8,9},{9,8},{10,11... | collective-permute-start | bytes 1179656 | tf_op jit(solution)/shard_map/ppermute | solution.py:284
  80.0 12.1 %collective-permute-start.20 = (bf16[64,3072]{1,0:T(8,128)(2,1)S(1)}, bf16[64,3072]{1,0:T(8,128)(2,1)S(1)}, u32[]{:S(2)}, u32[]{:S(2)}) collective-permute-start(bf16[64,3072]{1,0:T(8,128)(2,1)S(1)} %get-tuple-element.278.refs_0_), channel_id=1, source_target_pairs={{0,2},{1,3},{2,0},{3,1},{4,6},{5,7},{6,4},{7,5},{8,10},{9,11},{10,... | collective-permute-start | bytes 1179656 | tf_op jit(solution)/shard_map/ppermute | solution.py:287
  82.1 21.1 %collective-permute-start.18 = (bf16[128,3072]{1,0:T(8,128)(2,1)S(1)}, bf16[128,3072]{1,0:T(8,128)(2,1)S(1)}, u32[]{:S(2)}, u32[]{:S(2)}) collective-permute-start(bf16[128,3072]{1,0:T(8,128)(2,1)S(1)} %get-tuple-element.284.refs_0_), channel_id=1, source_target_pairs={{0,1},{1,0},{2,3},{3,2},{4,5},{5,4},{6,7},{7,6},{8,9},{9,8},{10,11... | collective-permute-start | bytes 2359304 | tf_op jit(solution)/shard_map/ppermute | solution.py:284
  83.7 25.2 %collective-permute-start.19 = (bf16[128,3072]{1,0:T(8,128)(2,1)S(1)}, bf16[128,3072]{1,0:T(8,128)(2,1)S(1)}, u32[]{:S(2)}, u32[]{:S(2)}) collective-permute-start(bf16[128,3072]{1,0:T(8,128)(2,1)S(1)} %get-tuple-element.286.refs_2_), channel_id=1, source_target_pairs={{0,2},{1,3},{2,0},{3,1},{4,6},{5,7},{6,4},{7,5},{8,10},{9,11},{10,... | collective-permute-start | bytes 2359304 | tf_op jit(solution)/shard_map/ppermute | solution.py:287
  92.0 18.6 %collective-permute-start.24 = (bf16[256,1536]{1,0:T(8,128)(2,1)S(1)}, bf16[256,1536]{1,0:T(8,128)(2,1)S(1)}, u32[]{:S(2)}, u32[]{:S(2)}) collective-permute-start(bf16[256,1536]{1,0:T(8,128)(2,1)S(1)} %collective-permute-done.17.mine_ref), channel_id=1, source_target_pairs={{0,4},{4,8},{8,12},{12,0},{1,5},{5,9},{9,13},{13,1},{2,6},{6,10},{... | collective-permute-start | bytes 2359304 | tf_op jit(solution)/shard_map/ppermute | solution.py:293
  94.2 31.5 %collective-permute-start.28 = (bf16[128,3072]{1,0:T(8,128)(2,1)S(1)}, bf16[128,3072]{1,0:T(8,128)(2,1)S(1)}, u32[]{:S(2)}, u32[]{:S(2)}) collective-permute-start(bf16[128,3072]{1,0:T(8,128)(2,1)S(1)} %get-tuple-element.306.refs_0_), channel_id=1, source_target_pairs={{0,1},{1,0},{2,3},{3,2},{4,5},{5,4},{6,7},{7,6},{8,9},{9,8},{10,11... | collective-permute-start | bytes 2359304 | tf_op jit(solution)/shard_map/ppermute | solution.py:284
  95.8 30.0 %collective-permute-start.29 = (bf16[128,3072]{1,0:T(8,128)(2,1)S(1)}, bf16[128,3072]{1,0:T(8,128)(2,1)S(1)}, u32[]{:S(2)}, u32[]{:S(2)}) collective-permute-start(bf16[128,3072]{1,0:T(8,128)(2,1)S(1)} %get-tuple-element.308.refs_2_), channel_id=1, source_target_pairs={{0,2},{1,3},{2,0},{3,1},{4,6},{5,7},{6,4},{7,5},{8,10},{9,11},{10,... | collective-permute-start | bytes 2359304 | tf_op jit(solution)/shard_map/ppermute | solution.py:287
  111.3 27.3 %collective-permute-start.32 = (bf16[128,3072]{1,0:T(8,128)(2,1)}, bf16[128,3072]{1,0:T(8,128)(2,1)S(1)}, u32[]{:S(2)}, u32[]{:S(2)}) collective-permute-start(bf16[128,3072]{1,0:T(8,128)(2,1)} %get-tuple-element.314), channel_id=1, source_target_pairs={{0,1},{1,0},{2,3},{3,2},{4,5},{5,4},{6,7},{7,6},{8,9},{9,8},{10,11... | collective-permute-start | bytes 2359304 | tf_op jit(solution)/shard_map/ppermute | solution.py:284
  112.5 30.1 %collective-permute-start.33 = (bf16[128,3072]{1,0:T(8,128)(2,1)}, bf16[128,3072]{1,0:T(8,128)(2,1)S(1)}, u32[]{:S(2)}, u32[]{:S(2)}) collective-permute-start(bf16[128,3072]{1,0:T(8,128)(2,1)} %get-tuple-element.315), channel_id=1, source_target_pairs={{0,2},{1,3},{2,0},{3,1},{4,6},{5,7},{6,4},{7,5},{8,10},{9,11},{10,... | collective-permute-start | bytes 2359304 | tf_op jit(solution)/shard_map/ppermute | solution.py:287
  126.4 27.3 %collective-permute-start.30 = (bf16[128,3072]{1,0:T(8,128)(2,1)}, bf16[128,3072]{1,0:T(8,128)(2,1)S(1)}, u32[]{:S(2)}, u32[]{:S(2)}) collective-permute-start(bf16[128,3072]{1,0:T(8,128)(2,1)} %get-tuple-element.312), channel_id=1, source_target_pairs={{0,1},{1,0},{2,3},{3,2},{4,5},{5,4},{6,7},{7,6},{8,9},{9,8},{10,11... | collective-permute-start | bytes 2359304 | tf_op jit(solution)/shard_map/ppermute | solution.py:284
  128.0 31.5 %collective-permute-start.31 = (bf16[128,3072]{1,0:T(8,128)(2,1)}, bf16[128,3072]{1,0:T(8,128)(2,1)S(1)}, u32[]{:S(2)}, u32[]{:S(2)}) collective-permute-start(bf16[128,3072]{1,0:T(8,128)(2,1)} %get-tuple-element.313), channel_id=1, source_target_pairs={{0,2},{1,3},{2,0},{3,1},{4,6},{5,7},{6,4},{7,5},{8,10},{9,11},{10,... | collective-permute-start | bytes 2359304 | tf_op jit(solution)/shard_map/ppermute | solution.py:287
  132.4 31.2 %collective-permute-start.42 = (f32[128,1536]{1,0:T(8,128)S(1)}, f32[128,1536]{1,0:T(8,128)S(1)}, u32[]{:S(2)}, u32[]{:S(2)}) collective-permute-start(f32[128,1536]{1,0:T(8,128)S(1)} %get-tuple-element.318), channel_id=1, source_target_pairs={{0,16},{16,0},{1,17},{17,1},{2,18},{18,2},{3,19},{19,3},{4,20},{20... | collective-permute-start | bytes 2359304 | tf_op jit(solution)/shard_map/ppermute | solution.py:290
  145.5 22.4 %collective-permute-start.36 = (bf16[64,3072]{1,0:T(8,128)(2,1)S(1)}, bf16[64,3072]{1,0:T(8,128)(2,1)S(1)}, u32[]{:S(2)}, u32[]{:S(2)}) collective-permute-start(bf16[64,3072]{1,0:T(8,128)(2,1)S(1)} %get-tuple-element.327), channel_id=1, source_target_pairs={{0,2},{1,3},{2,0},{3,1},{4,6},{5,7},{6,4},{7,5},{8,10},{9,11},{10,... | collective-permute-start | bytes 1179656 | tf_op jit(solution)/shard_map/ppermute | solution.py:287
  147.3 20.6 %collective-permute-start.37 = (bf16[64,3072]{1,0:T(8,128)(2,1)S(1)}, bf16[64,3072]{1,0:T(8,128)(2,1)S(1)}, u32[]{:S(2)}, u32[]{:S(2)}) collective-permute-start(bf16[64,3072]{1,0:T(8,128)(2,1)S(1)} %get-tuple-element.329), channel_id=1, source_target_pairs={{0,1},{1,0},{2,3},{3,2},{4,5},{5,4},{6,7},{7,6},{8,9},{9,8},{10,11... | collective-permute-start | bytes 1179656 | tf_op jit(solution)/shard_map/ppermute | solution.py:284
  160.3 16.0 %collective-permute-start.34 = (bf16[64,3072]{1,0:T(8,128)(2,1)S(1)}, bf16[64,3072]{1,0:T(8,128)(2,1)S(1)}, u32[]{:S(2)}, u32[]{:S(2)}) collective-permute-start(bf16[64,3072]{1,0:T(8,128)(2,1)S(1)} %get-tuple-element.336), channel_id=1, source_target_pairs={{0,2},{1,3},{2,0},{3,1},{4,6},{5,7},{6,4},{7,5},{8,10},{9,11},{10,... | collective-permute-start | bytes 1179656 | tf_op jit(solution)/shard_map/ppermute | solution.py:287
  162.1 14.2 %collective-permute-start.35 = (bf16[64,3072]{1,0:T(8,128)(2,1)S(1)}, bf16[64,3072]{1,0:T(8,128)(2,1)S(1)}, u32[]{:S(2)}, u32[]{:S(2)}) collective-permute-start(bf16[64,3072]{1,0:T(8,128)(2,1)S(1)} %get-tuple-element.338), channel_id=1, source_target_pairs={{0,1},{1,0},{2,3},{3,2},{4,5},{5,4},{6,7},{7,6},{8,9},{9,8},{10,11... | collective-permute-start | bytes 1179656 | tf_op jit(solution)/shard_map/ppermute | solution.py:284
  163.9 33.6 %collective-permute-start.43 = (f32[128,1536]{1,0:T(8,128)S(1)}, f32[128,1536]{1,0:T(8,128)S(1)}, u32[]{:S(2)}, u32[]{:S(2)}) collective-permute-start(f32[128,1536]{1,0:T(8,128)S(1)} %add.3), channel_id=1, source_target_pairs={{0,4},{4,8},{8,12},{12,0},{1,5},{5,9},{9,13},{13,1},{2,6},{6,10},{... | collective-permute-start | bytes 2359304 | tf_op jit(solution)/shard_map/ppermute | solution.py:293
  168.8 11.7 %collective-permute-start.41 = (bf16[64,3072]{1,0:T(8,128)(2,1)S(1)}, bf16[64,3072]{1,0:T(8,128)(2,1)S(1)}, u32[]{:S(2)}, u32[]{:S(2)}) collective-permute-start(bf16[64,3072]{1,0:T(8,128)(2,1)S(1)} %get-tuple-element.353.refs_2_), channel_id=1, source_target_pairs={{0,1},{1,0},{2,3},{3,2},{4,5},{5,4},{6,7},{7,6},{8,9},{9,8},{10,11... | collective-permute-start | bytes 1179656 | tf_op jit(solution)/shard_map/ppermute | solution.py:284
  170.4 14.3 %collective-permute-start.40 = (bf16[64,3072]{1,0:T(8,128)(2,1)S(1)}, bf16[64,3072]{1,0:T(8,128)(2,1)S(1)}, u32[]{:S(2)}, u32[]{:S(2)}) collective-permute-start(bf16[64,3072]{1,0:T(8,128)(2,1)S(1)} %get-tuple-element.351.refs_0_), channel_id=1, source_target_pairs={{0,2},{1,3},{2,0},{3,1},{4,6},{5,7},{6,4},{7,5},{8,10},{9,11},{10,... | collective-permute-start | bytes 1179656 | tf_op jit(solution)/shard_map/ppermute | solution.py:287
  177.2 20.3 %collective-permute-start.38 = (bf16[64,3072]{1,0:T(8,128)(2,1)S(1)}, bf16[64,3072]{1,0:T(8,128)(2,1)S(1)}, u32[]{:S(2)}, u32[]{:S(2)}) collective-permute-start(bf16[64,3072]{1,0:T(8,128)(2,1)S(1)} %get-tuple-element.361.refs_0_), channel_id=1, source_target_pairs={{0,2},{1,3},{2,0},{3,1},{4,6},{5,7},{6,4},{7,5},{8,10},{9,11},{10,... | collective-permute-start | bytes 1179656 | tf_op jit(solution)/shard_map/ppermute | solution.py:287
  179.1 18.5 %collective-permute-start.39 = (bf16[64,3072]{1,0:T(8,128)(2,1)S(1)}, bf16[64,3072]{1,0:T(8,128)(2,1)S(1)}, u32[]{:S(2)}, u32[]{:S(2)}) collective-permute-start(bf16[64,3072]{1,0:T(8,128)(2,1)S(1)} %get-tuple-element.363.refs_2_), channel_id=1, source_target_pairs={{0,1},{1,0},{2,3},{3,2},{4,5},{5,4},{6,7},{7,6},{8,9},{9,8},{10,11... | collective-permute-start | bytes 1179656 | tf_op jit(solution)/shard_map/ppermute | solution.py:284
  185.1 21.9 %collective-permute-start.46 = (bf16[128,3072]{1,0:T(8,128)(2,1)S(1)}, bf16[128,3072]{1,0:T(8,128)(2,1)S(1)}, u32[]{:S(2)}, u32[]{:S(2)}) collective-permute-start(bf16[128,3072]{1,0:T(8,128)(2,1)S(1)} %get-tuple-element.367.refs_0_), channel_id=1, source_target_pairs={{0,1},{1,0},{2,3},{3,2},{4,5},{5,4},{6,7},{7,6},{8,9},{9,8},{10,11... | collective-permute-start | bytes 2359304 | tf_op jit(solution)/shard_map/ppermute | solution.py:284
  186.7 23.3 %collective-permute-start.47 = (bf16[128,3072]{1,0:T(8,128)(2,1)S(1)}, bf16[128,3072]{1,0:T(8,128)(2,1)S(1)}, u32[]{:S(2)}, u32[]{:S(2)}) collective-permute-start(bf16[128,3072]{1,0:T(8,128)(2,1)S(1)} %get-tuple-element.369.refs_2_), channel_id=1, source_target_pairs={{0,2},{1,3},{2,0},{3,1},{4,6},{5,7},{6,4},{7,5},{8,10},{9,11},{10,... | collective-permute-start | bytes 2359304 | tf_op jit(solution)/shard_map/ppermute | solution.py:287
  197.9 22.6 %collective-permute-start.44 = (bf16[128,3072]{1,0:T(8,128)(2,1)S(1)}, bf16[128,3072]{1,0:T(8,128)(2,1)S(1)}, u32[]{:S(2)}, u32[]{:S(2)}) collective-permute-start(bf16[128,3072]{1,0:T(8,128)(2,1)S(1)} %get-tuple-element.381.refs_0_), channel_id=1, source_target_pairs={{0,1},{1,0},{2,3},{3,2},{4,5},{5,4},{6,7},{7,6},{8,9},{9,8},{10,11... | collective-permute-start | bytes 2359304 | tf_op jit(solution)/shard_map/ppermute | solution.py:284
  198.5 26.2 %collective-permute-start.45 = (bf16[128,3072]{1,0:T(8,128)(2,1)S(1)}, bf16[128,3072]{1,0:T(8,128)(2,1)S(1)}, u32[]{:S(2)}, u32[]{:S(2)}) collective-permute-start(bf16[128,3072]{1,0:T(8,128)(2,1)S(1)} %get-tuple-element.383.refs_2_), channel_id=1, source_target_pairs={{0,2},{1,3},{2,0},{3,1},{4,6},{5,7},{6,4},{7,5},{8,10},{9,11},{10,... | collective-permute-start | bytes 2359304 | tf_op jit(solution)/shard_map/ppermute | solution.py:287
  216.9 21.7 %collective-permute-start.52 = (f32[128,1536]{1,0:T(8,128)}, f32[128,1536]{1,0:T(8,128)}, u32[]{:S(2)}, u32[]{:S(2)}) collective-permute-start(f32[128,1536]{1,0:T(8,128)} %add.4), channel_id=1, source_target_pairs={{0,4},{4,8},{8,12},{12,0},{1,5},{5,9},{9,13},{13,1},{2,6},{6,10},{... | collective-permute-start | bytes 2359304 | tf_op jit(solution)/shard_map/ppermute | solution.py:293
  229.6 8.1 %collective-permute-start.50 = (f32[64,1536]{1,0:T(8,128)}, f32[64,1536]{1,0:T(8,128)S(1)}, u32[]{:S(2)}, u32[]{:S(2)}) collective-permute-start(f32[64,1536]{1,0:T(8,128)} %get-tuple-element.389), channel_id=1, source_target_pairs={{0,16},{16,0},{1,17},{17,1},{2,18},{18,2},{3,19},{19,3},{4,20},{20... | collective-permute-start | bytes 1179656 | tf_op jit(solution)/shard_map/ppermute | solution.py:290
  229.6 8.1 %collective-permute-start.51 = (f32[64,1536]{1,0:T(8,128)S(1)}, f32[64,1536]{1,0:T(8,128)S(1)}, u32[]{:S(2)}, u32[]{:S(2)}) collective-permute-start(f32[64,1536]{1,0:T(8,128)S(1)} %get-tuple-element.390), channel_id=1, source_target_pairs={{0,16},{16,0},{1,17},{17,1},{2,18},{18,2},{3,19},{19,3},{4,20},{20... | collective-permute-start | bytes 1179656 | tf_op jit(solution)/shard_map/ppermute | solution.py:290
  230.1 19.0 %collective-permute-start.27 = (f32[128,1536]{1,0:T(8,128)}, f32[128,1536]{1,0:T(8,128)S(1)}, u32[]{:S(2)}, u32[]{:S(2)}) collective-permute-start(f32[128,1536]{1,0:T(8,128)} %get-tuple-element.305), channel_id=1, source_target_pairs={{0,16},{16,0},{1,17},{17,1},{2,18},{18,2},{3,19},{19,3},{4,20},{20... | collective-permute-start | bytes 2359304 | tf_op jit(solution)/shard_map/ppermute | solution.py:290
  240.7 12.6 %collective-permute-start.53 = (bf16[128,1536]{1,0:T(8,128)(2,1)S(1)}, bf16[128,1536]{1,0:T(8,128)(2,1)S(1)}, u32[]{:S(2)}, u32[]{:S(2)}) collective-permute-start(bf16[128,1536]{1,0:T(8,128)(2,1)S(1)} %add.5), channel_id=1, source_target_pairs={{0,4},{4,8},{8,12},{12,0},{1,5},{5,9},{9,13},{13,1},{2,6},{6,10},{... | collective-permute-start | bytes 1179656 | tf_op jit(solution)/shard_map/ppermute | solution.py:293
  (39 other events, 293.2 us)
where the time goes:
time: 259 us; the launch traced here: 255 us
  waiting for transfers between devices  96.7 us (37%)
  Pallas kernels  84.2 us (33%)
  starting transfers between devices  60.7 us (23%)
  local copies, waits for them, and re-layouts  11.4 us (4%)
    pallas_call x41, Pallas kernels, call(): pl.pallas_call(body, grid=grid, in_specs=in_specs, out_specs=out_specs, o...  84.2 us
    ppermute x17, waiting for transfers between devices, swap_y(): return lax.ppermute(a, 'col', [(i, i ^ 2) for i in range(n_col)])  49.2 us
    ppermute x17, waiting for transfers between devices, swap_x(): return lax.ppermute(a, 'col', [(i, i ^ 1) for i in range(n_col)])  34.3 us
    ppermute x17, starting transfers between devices, swap_y(): return lax.ppermute(a, 'col', [(i, i ^ 2) for i in range(n_col)])  24.5 us
    ppermute x17, starting transfers between devices, swap_x(): return lax.ppermute(a, 'col', [(i, i ^ 1) for i in range(n_col)])  22.3 us
    unnamed x66, local copies, waits for them, and re-layouts  11.3 us
    ppermute x6, starting transfers between devices, pass_row(): return lax.ppermute(a, 'row', [(i, (i + 1) % n_row) for i in range(n_row)])  10.4 us
    ppermute x6, waiting for transfers between devices, pass_row(): return lax.ppermute(a, 'row', [(i, (i + 1) % n_row) for i in range(n_row)])  9.12 us
  transfers between devices with their start and end apart: 54, of which 26 were waited for; matrix products, arithmetic and copies ran while one was open for 0% of the time, Pallas kernels for 32%

commit v1 on v0

--- a/solution.py
+++ b/solution.py
@@ -479,7 +479,7 @@
         elif at == 1:
             running = pass_row(add_kernel(f32, w["part"], *w["part_came"]))
         else:
-            total = add_kernel(b16 if at == 3 else f32, *after(w["part"], *w["part_came"], running))
+            total = add_kernel(b16, *after(w["part"], *w["part_came"], running))
             token = (total,)
             running = pass_row(total)
 
@@ -548,8 +548,8 @@
     share_sum(2)
     join(3)
     share(3)
+    share_sum(3)
     up_grad = late(("in", "delta"), up_partial, True, "up_grad")
-    share_sum(3)
     down_grad = late(("active", "cot"), down_partial, False, "down_grad")
 
     def end_kernel(*arrays):

time: 259 us -> 255 us (0.985)
  waiting for transfers between devices: 96.7 us -> 91.2 us
  starting transfers between devices: 60.7 us -> 65.2 us
  Pallas kernels: 84.2 us -> 80.8 us
    ppermute x17, waiting for transfers between devices: 49.2 us -> 16.8 us  [swap_y(): return lax.ppermute(a, 'col', [(i, i ^ 2) for i in range(n_col)])]
    ppermute x17, waiting for transfers between devices: 34.3 us -> 65.7 us  [swap_x(): return lax.ppermute(a, 'col', [(i, i ^ 1) for i in range(n_col)])]
    ppermute x6, waiting for transfers between devices: 9.12 us -> 4.67 us  [pass_row(): return lax.ppermute(a, 'row', [(i, (i + 1) % n_row) for i in range(n_row)])]
    ppermute x17, starting transfers between devices: 24.5 us -> 28.1 us  [swap_y(): return lax.ppermute(a, 'col', [(i, i ^ 2) for i in range(n_col)])]
    pallas_call x41, Pallas kernels: 84.2 us -> 80.8 us  [call(): pl.pallas_call(body, grid=grid, in_specs=in_specs, out_specs=out_specs, o...]
    unnamed x66 -> x62, local copies, waits for them, and re-layouts: 11.3 us -> 11.5 us
  transfers between devices with their start and end apart: 54 -> 54, of which waited for: 26 -> 23; matrix products, arithmetic and copies ran while one was open for 0% -> 0% of each run, Pallas kernels for 32% -> 31%
where the time goes in v1:
time: 255 us; the launch traced here: 251 us
  waiting for transfers between devices  91.2 us (36%)
  Pallas kernels  80.8 us (32%)
  starting transfers between devices  65.2 us (26%)
  local copies, waits for them, and re-layouts  11.6 us (5%)
    pallas_call x41, Pallas kernels, call(): pl.pallas_call(body, grid=grid, in_specs=in_specs, out_specs=out_specs, o...  80.8 us
    ppermute x17, waiting for transfers between devices, swap_x(): return lax.ppermute(a, 'col', [(i, i ^ 1) for i in range(n_col)])  65.7 us
    ppermute x17, starting transfers between devices, swap_y(): return lax.ppermute(a, 'col', [(i, i ^ 2) for i in range(n_col)])  28.1 us
    ppermute x17, starting transfers between devices, swap_x(): return lax.ppermute(a, 'col', [(i, i ^ 1) for i in range(n_col)])  22.2 us
    ppermute x17, waiting for transfers between devices, swap_y(): return lax.ppermute(a, 'col', [(i, i ^ 2) for i in range(n_col)])  16.8 us
    unnamed x62, local copies, waits for them, and re-layouts  11.5 us
    ppermute x6, starting transfers between devices, pass_row(): return lax.ppermute(a, 'row', [(i, (i + 1) % n_row) for i in range(n_row)])  11.3 us
  transfers between devices with their start and end apart: 54, of which 23 were waited for; matrix products, arithmetic and copies ran while one was open for 0% of the time, Pallas kernels for 31%

profile of v1, /device:TPU:0, one launch (start us, length us, event | category | flops | bytes accessed | tf_op | source)
XLA Modules:
  0.0 250.6 jit_solution(6470014396929970826)
XLA Ops:
  2.4 2.6 %collective-permute-start.1 = (bf16[256,1536]{1,0:T(8,128)(2,1)S(1)}, bf16[256,1536]{1,0:T(8,128)(2,1)S(1)}, u32[]{:S(2)}, u32[]{:S(2)}) collective-permute-start(bf16[256,1536]{1,0:T(8,128)(2,1)S(1)} %reorder.1.mine_ref), channel_id=1, source_target_pairs={{0,4},{4,8},{8,12},{12,0},{1,5},{5,9},{9,13},{13,1},{2,6},{6,10},{... | collective-permute-start | bytes 2359304 | tf_op jit(solution)/shard_map/ppermute | solution.py:293
  5.2 3.7 %copy-done = bf16[1536,3072]{1,0:T(8,128)(2,1)S(1)} copy-done((bf16[1536,3072]{1,0:T(8,128)(2,1)S(1)}, bf16[1536,3072]{1,0:T(8,128)(2,1)}, u32[]{:S(2)}) %copy-start) | copy-done | bytes 9437208
  8.9 2.6 %hidden_product.4 = (f32[128,3072]{1,0:T(8,128)S(1)}, bf16[128,1536]{1,0:T(8,128)(2,1)S(1)}, bf16[128,1536]{1,0:T(8,128)(2,1)S(1)}) custom-call(bf16[256,1536]{1,0:T(8,128)(2,1)S(1)} %get-tuple-element.319.chunk_ref.refs_0_, bf16[1536,3072]{1,0:T(8,128)(2,1)S(1)} %copy-done), custom_call_target="tpu_custom_call" | custom-call | flops 1000 | bytes 1000 | tf_op jit(solution)/shard_map/hidden_product/pallas_call | solution.py:30
  11.5 2.2 collective-permute-start.2
  15.2 3.7 %copy-done.1 = bf16[3072,1536]{1,0:T(8,128)(2,1)S(1)} copy-done((bf16[3072,1536]{1,0:T(8,128)(2,1)S(1)}, bf16[3072,1536]{1,0:T(8,128)(2,1)}, u32[]{:S(2)}) %copy-start.1) | copy-done | bytes 9437208
  18.9 2.6 %delta_act_product.4 = (f32[128,3072]{1,0:T(8,128)S(1)}, bf16[128,1536]{1,0:T(8,128)(2,1)S(1)}, bf16[128,1536]{1,0:T(8,128)(2,1)S(1)}) custom-call(bf16[256,1536]{1,0:T(8,128)(2,1)S(1)} %get-tuple-element.359.chunk_ref.refs_2_, bf16[3072,1536]{1,0:T(8,128)(2,1)S(1)} %copy-done.1), custom_call_target="tpu_custom_call" | custom-call | flops 1000 | bytes 1000 | tf_op jit(solution)/shard_map/delta_act_product/pallas_call | solution.py:30
  22.2 3.1 %collective-permute-done.1.mine_ref = bf16[256,1536]{1,0:T(8,128)(2,1)S(1)} collective-permute-done((bf16[256,1536]{1,0:T(8,128)(2,1)S(1)}, bf16[256,1536]{1,0:T(8,128)(2,1)S(1)}, u32[]{:S(2)}, u32[]{:S(2)}) %collective-permute-start.1) | collective-permute-done | bytes 786464 | tf_op jit(solution)/shard_map/ppermute | solution.py:293
  29.6 2.6 %hidden_product.5 = (f32[128,3072]{1,0:T(8,128)S(1)}, bf16[128,3072]{1,0:T(8,128)(2,1)S(1)}) custom-call(bf16[256,1536]{1,0:T(8,128)(2,1)S(1)} %get-tuple-element.320.chunk_ref.refs_1_, bf16[1536,3072]{1,0:T(8,128)(2,1)S(1)} %bitcast.2), custom_call_target="tpu_custom_call" | custom-call | flops 1000 | bytes 1000 | tf_op jit(solution)/shard_map/hidden_product/pallas_call | solution.py:30
  32.8 2.6 %delta_act_product.5 = (f32[128,3072]{1,0:T(8,128)S(1)}, bf16[128,3072]{1,0:T(8,128)(2,1)S(1)}) custom-call(bf16[256,1536]{1,0:T(8,128)(2,1)S(1)} %get-tuple-element.360.chunk_ref.refs_3_, bf16[3072,1536]{1,0:T(8,128)(2,1)S(1)} %bitcast.4), custom_call_target="tpu_custom_call" | custom-call | flops 1000 | bytes 1000 | tf_op jit(solution)/shard_map/delta_act_product/pallas_call | solution.py:30
  35.4 2.0 collective-permute-start.12
  39.3 13.3 %collective-permute-done.11.ch = bf16[128,3072]{1,0:T(8,128)(2,1)S(1)} collective-permute-done((bf16[128,3072]{1,0:T(8,128)(2,1)S(1)}, bf16[128,3072]{1,0:T(8,128)(2,1)S(1)}, u32[]{:S(2)}, u32[]{:S(2)}) %collective-permute-start.11) | collective-permute-done | bytes 786464 | tf_op jit(solution)/shard_map/ppermute | solution.py:284
  52.7 3.3 %collective-permute-done.12.cg = bf16[128,3072]{1,0:T(8,128)(2,1)S(1)} collective-permute-done((bf16[128,3072]{1,0:T(8,128)(2,1)S(1)}, bf16[128,3072]{1,0:T(8,128)(2,1)S(1)}, u32[]{:S(2)}, u32[]{:S(2)}) %collective-permute-start.12) | collective-permute-done | bytes 786464 | tf_op jit(solution)/shard_map/ppermute | solution.py:287
  56.8 2.0 collective-permute-start.15
  60.3 4.1 %collective-permute-done.9.ch = bf16[64,3072]{1,0:T(8,128)(2,1)S(1)} collective-permute-done((bf16[64,3072]{1,0:T(8,128)(2,1)S(1)}, bf16[64,3072]{1,0:T(8,128)(2,1)S(1)}, u32[]{:S(2)}, u32[]{:S(2)}) %collective-permute-start.9) | collective-permute-done | bytes 393248 | tf_op jit(solution)/shard_map/ppermute | solution.py:287
  65.4 2.0 collective-permute-start.13
  68.9 3.9 %collective-permute-done.15.ch = bf16[64,3072]{1,0:T(8,128)(2,1)S(1)} collective-permute-done((bf16[64,3072]{1,0:T(8,128)(2,1)S(1)}, bf16[64,3072]{1,0:T(8,128)(2,1)S(1)}, u32[]{:S(2)}, u32[]{:S(2)}) %collective-permute-start.15) | collective-permute-done | bytes 393248 | tf_op jit(solution)/shard_map/ppermute | solution.py:287
  74.4 1.9 collective-permute-start.20
  76.3 4.9 %collective-permute-done.13.refs_1_ = bf16[64,3072]{1,0:T(8,128)(2,1)S(1)} collective-permute-done((bf16[64,3072]{1,0:T(8,128)(2,1)S(1)}, bf16[64,3072]{1,0:T(8,128)(2,1)S(1)}, u32[]{:S(2)}, u32[]{:S(2)}) %collective-permute-start.13) | collective-permute-done | bytes 393248 | tf_op jit(solution)/shard_map/ppermute | solution.py:287
  83.7 1.9 collective-permute-start.19
  85.8 3.5 %hidden_product.6 = (f32[128,3072]{1,0:T(8,128)S(1)}, bf16[128,3072]{1,0:T(8,128)(2,1)}) custom-call(bf16[256,1536]{1,0:T(8,128)(2,1)S(1)} %get-tuple-element.395.chunk_ref.refs_0_, bf16[1536,3072]{1,0:T(8,128)(2,1)S(1)} %bitcast.2), custom_call_target="tpu_custom_call" | custom-call | flops 1000 | bytes 1000 | tf_op jit(solution)/shard_map/hidden_product/pallas_call | solution.py:30
  89.3 3.5 %delta_act_product.6 = (f32[128,3072]{1,0:T(8,128)S(1)}, bf16[128,3072]{1,0:T(8,128)(2,1)}) custom-call(bf16[256,1536]{1,0:T(8,128)(2,1)S(1)} %get-tuple-element.401.chunk_ref.refs_2_, bf16[3072,1536]{1,0:T(8,128)(2,1)S(1)} %bitcast.4), custom_call_target="tpu_custom_call" | custom-call | flops 1000 | bytes 1000 | tf_op jit(solution)/shard_map/delta_act_product/pallas_call | solution.py:30
  97.0 1.9 collective-permute-start.29
  98.9 11.2 %collective-permute-done.18.refs_1_ = bf16[128,3072]{1,0:T(8,128)(2,1)S(1)} collective-permute-done((bf16[128,3072]{1,0:T(8,128)(2,1)S(1)}, bf16[128,3072]{1,0:T(8,128)(2,1)S(1)}, u32[]{:S(2)}, u32[]{:S(2)}) %collective-permute-start.18) | collective-permute-done | bytes 786464 | tf_op jit(solution)/shard_map/ppermute | solution.py:284
  113.0 1.9 collective-permute-start.33
  115.0 3.5 %hidden_product.7 = (f32[128,3072]{1,0:T(8,128)S(1)}, bf16[128,3072]{1,0:T(8,128)(2,1)}) custom-call(bf16[256,1536]{1,0:T(8,128)(2,1)S(1)} %get-tuple-element.396.chunk_ref.refs_1_, bf16[1536,3072]{1,0:T(8,128)(2,1)S(1)} %bitcast.2), custom_call_target="tpu_custom_call" | custom-call | flops 1000 | bytes 1000 | tf_op jit(solution)/shard_map/hidden_product/pallas_call | solution.py:30
  118.6 3.5 %delta_act_product.7 = (f32[128,3072]{1,0:T(8,128)S(1)}, bf16[128,3072]{1,0:T(8,128)(2,1)}) custom-call(bf16[256,1536]{1,0:T(8,128)(2,1)S(1)} %get-tuple-element.402.chunk_ref.refs_3_, bf16[3072,1536]{1,0:T(8,128)(2,1)S(1)} %bitcast.4), custom_call_target="tpu_custom_call" | custom-call | flops 1000 | bytes 1000 | tf_op jit(solution)/shard_map/delta_act_product/pallas_call | solution.py:30
  122.1 3.5 %input_product.4 = (f32[128,1536]{1,0:T(8,128)S(1)}, f32[128,1536]{1,0:T(8,128)}) custom-call(bf16[256,3072]{1,0:T(8,128)(2,1)S(1)} %get-tuple-element.321.delta_ref.refs_2_, bf16[1536,3072]{1,0:T(8,128)(2,1)S(1)} %bitcast.2), custom_call_target="tpu_custom_call" | custom-call | flops 1000 | bytes 1000 | tf_op jit(solution)/shard_map/input_product/pallas_call | solution.py:30
  129.2 1.9 collective-permute-start.31
  131.2 2.6 %input_product.5 = (f32[128,1536]{1,0:T(8,128)S(1)}, f32[128,1536]{1,0:T(8,128)S(1)}) custom-call(bf16[256,3072]{1,0:T(8,128)(2,1)S(1)} %get-tuple-element.322.delta_ref.refs_3_, bf16[1536,3072]{1,0:T(8,128)(2,1)S(1)} %bitcast.2), custom_call_target="tpu_custom_call" | custom-call | flops 1000 | bytes 1000 | tf_op jit(solution)/shard_map/input_product/pallas_call | solution.py:30
  133.9 6.1 %up_grad_early.1.refs_4_ = f32[1536,3072]{1,0:T(8,128)S(1)} custom-call(bf16[256,1536]{1,0:T(8,128)(2,1)S(1)} %get-tuple-element.319.chunk_ref.refs_0_, bf16[256,1536]{1,0:T(8,128)(2,1)S(1)} %get-tuple-element.320.chunk_ref.refs_1_, bf16[256,3072]{1,0:T(8,128)(2,1)S(1)} %get-tuple-element.321.delta_ref.refs_2_, ...), custom_call_target="tpu_custom_call" | custom-call | flops 1000 | bytes 1000 | tf_op jit(solution)/shard_map/up_grad_early/pallas_call | solution.py:30
  140.0 3.8 %collective-permute-done.32.ch = bf16[128,3072]{1,0:T(8,128)(2,1)S(1)} collective-permute-done((bf16[128,3072]{1,0:T(8,128)(2,1)}, bf16[128,3072]{1,0:T(8,128)(2,1)S(1)}, u32[]{:S(2)}, u32[]{:S(2)}) %collective-permute-start.32) | collective-permute-done | bytes 786464 | tf_op jit(solution)/shard_map/ppermute | solution.py:284
  146.7 2.0 collective-permute-start.36
  150.2 10.5 %collective-permute-done.30.ch = bf16[128,3072]{1,0:T(8,128)(2,1)S(1)} collective-permute-done((bf16[128,3072]{1,0:T(8,128)(2,1)}, bf16[128,3072]{1,0:T(8,128)(2,1)S(1)}, u32[]{:S(2)}, u32[]{:S(2)}) %collective-permute-start.30) | collective-permute-done | bytes 786464 | tf_op jit(solution)/shard_map/ppermute | solution.py:284
  161.6 2.0 collective-permute-start.34
  165.4 1.9 collective-permute-start.43
  167.3 1.8 collective-permute-done.37.cg
  170.1 2.0 collective-permute-start.40
  173.9 3.6 %collective-permute-done.35.cg = bf16[64,3072]{1,0:T(8,128)(2,1)S(1)} collective-permute-done((bf16[64,3072]{1,0:T(8,128)(2,1)S(1)}, bf16[64,3072]{1,0:T(8,128)(2,1)S(1)}, u32[]{:S(2)}, u32[]{:S(2)}) %collective-permute-start.35) | collective-permute-done | bytes 393248 | tf_op jit(solution)/shard_map/ppermute | solution.py:284
  178.5 2.0 collective-permute-start.38
  182.3 3.6 %collective-permute-done.41.refs_3_ = bf16[64,3072]{1,0:T(8,128)(2,1)S(1)} collective-permute-done((bf16[64,3072]{1,0:T(8,128)(2,1)S(1)}, bf16[64,3072]{1,0:T(8,128)(2,1)S(1)}, u32[]{:S(2)}, u32[]{:S(2)}) %collective-permute-start.41) | collective-permute-done | bytes 393248 | tf_op jit(solution)/shard_map/ppermute | solution.py:284
  187.9 1.9 collective-permute-start.47
  189.9 9.1 %down_grad_early.1.refs_4_ = f32[3072,1536]{1,0:T(8,128)} custom-call(bf16[256,3072]{1,0:T(8,128)(2,1)S(1)} %get-tuple-element.357.refs_0_, bf16[256,3072]{1,0:T(8,128)(2,1)S(1)} %get-tuple-element.358.refs_1_, bf16[256,1536]{1,0:T(8,128)(2,1)S(1)} %get-tuple-element.359.chunk_ref.refs_2_, bf16[256,1536]{1,0:T(8,128)(2,1)S(1)} %get-tuple-element.360.chunk_ref.refs_3_), custom_call_target="tpu_custom_call" | custom-call | flops 1000 | bytes 1000 | tf_op jit(solution)/shard_map/down_grad_early/pallas_call | solution.py:30
  200.1 11.2 %collective-permute-done.46.refs_1_ = bf16[128,3072]{1,0:T(8,128)(2,1)S(1)} collective-permute-done((bf16[128,3072]{1,0:T(8,128)(2,1)S(1)}, bf16[128,3072]{1,0:T(8,128)(2,1)S(1)}, u32[]{:S(2)}, u32[]{:S(2)}) %collective-permute-start.46) | collective-permute-done | bytes 786464 | tf_op jit(solution)/shard_map/ppermute | solution.py:284
  212.0 2.6 %input_product.6 = (f32[128,1536]{1,0:T(8,128)S(1)}, f32[64,1536]{1,0:T(8,128)S(1)}, f32[64,1536]{1,0:T(8,128)S(1)}) custom-call(bf16[256,3072]{1,0:T(8,128)(2,1)S(1)} %get-tuple-element.397.delta_ref.refs_2_, bf16[1536,3072]{1,0:T(8,128)(2,1)S(1)} %bitcast.2), custom_call_target="tpu_custom_call" | custom-call | flops 1000 | bytes 1000 | tf_op jit(solution)/shard_map/input_product/pallas_call | solution.py:30
  218.9 5.8 %collective-permute-done.44.refs_1_ = bf16[128,3072]{1,0:T(8,128)(2,1)S(1)} collective-permute-done((bf16[128,3072]{1,0:T(8,128)(2,1)S(1)}, bf16[128,3072]{1,0:T(8,128)(2,1)S(1)}, u32[]{:S(2)}, u32[]{:S(2)}) %collective-permute-start.44) | collective-permute-done | bytes 786464 | tf_op jit(solution)/shard_map/ppermute | solution.py:284
  225.4 2.6 %input_product.7 = (f32[128,1536]{1,0:T(8,128)S(1)}, f32[64,1536]{1,0:T(8,128)S(1)}, f32[64,1536]{1,0:T(8,128)S(1)}) custom-call(bf16[256,3072]{1,0:T(8,128)(2,1)S(1)} %get-tuple-element.398.delta_ref.refs_3_, bf16[1536,3072]{1,0:T(8,128)(2,1)S(1)} %bitcast.2), custom_call_target="tpu_custom_call" | custom-call | flops 1000 | bytes 1000 | tf_op jit(solution)/shard_map/input_product/pallas_call | solution.py:30
  233.0 7.5 %up_grad.1 = bf16[1536,3072]{1,0:T(8,128)(2,1)} custom-call(bf16[256,1536]{1,0:T(8,128)(2,1)S(1)} %get-tuple-element.395.chunk_ref.refs_0_, bf16[256,1536]{1,0:T(8,128)(2,1)S(1)} %copy-done.3, bf16[256,3072]{1,0:T(8,128)(2,1)S(1)} %get-tuple-element.397.delta_ref.refs_2_, bf16[256,3072]{1,0:T(8,128)(2,1)S(1)} %get-tuple-element.398.delta_ref.refs_3_, ...), custom_call_target="tpu_custom_call" | custom-call | flops 1000 | bytes 1000 | tf_op jit(solution)/shard_map/up_grad/pallas_call | solution.py:30
  241.6 7.5 %down_grad.1 = bf16[3072,1536]{1,0:T(8,128)(2,1)} custom-call(bf16[256,3072]{1,0:T(8,128)(2,1)S(1)} %copy-done.5, bf16[256,3072]{1,0:T(8,128)(2,1)S(1)} %copy-done.7, bf16[256,1536]{1,0:T(8,128)(2,1)S(1)} %get-tuple-element.401.chunk_ref.refs_2_, bf16[256,1536]{1,0:T(8,128)(2,1)S(1)} %get-tuple-element.402.chunk_ref.refs_3_, f32[3072,1536]{1,0:T(8,128)S(1)} %bitcast.6), custom_call_target="tpu_custom_call" | custom-call | flops 1000 | bytes 1000 | tf_op jit(solution)/shard_map/down_grad/pallas_call | solution.py:30
  (170 shorter events, 59.0 us)
Async XLA Ops:
  1.9 3.2 %collective-permute-start = (bf16[256,1536]{1,0:T(8,128)(2,1)S(1)}, bf16[256,1536]{1,0:T(8,128)(2,1)S(1)}, u32[]{:S(2)}, u32[]{:S(2)}) collective-permute-start(bf16[256,1536]{1,0:T(8,128)(2,1)S(1)} %reorder.1.mine_ref), channel_id=1, source_target_pairs={{0,16},{16,0},{1,17},{17,1},{2,18},{18,2},{3,19},{19,3},{4,20},{20... | collective-permute-start | bytes 2359304 | tf_op jit(solution)/shard_map/ppermute | solution.py:290
  2.4 22.8 %collective-permute-start.1 = (bf16[256,1536]{1,0:T(8,128)(2,1)S(1)}, bf16[256,1536]{1,0:T(8,128)(2,1)S(1)}, u32[]{:S(2)}, u32[]{:S(2)}) collective-permute-start(bf16[256,1536]{1,0:T(8,128)(2,1)S(1)} %reorder.1.mine_ref), channel_id=1, source_target_pairs={{0,4},{4,8},{8,12},{12,0},{1,5},{5,9},{9,13},{13,1},{2,6},{6,10},{... | collective-permute-start | bytes 2359304 | tf_op jit(solution)/shard_map/ppermute | solution.py:293
  11.5 13.8 %collective-permute-start.2 = (bf16[128,1536]{1,0:T(8,128)(2,1)S(1)}, bf16[128,1536]{1,0:T(8,128)(2,1)S(1)}, u32[]{:S(2)}, u32[]{:S(2)}) collective-permute-start(bf16[128,1536]{1,0:T(8,128)(2,1)S(1)} %get-tuple-element.209), channel_id=1, source_target_pairs={{0,1},{1,0},{2,3},{3,2},{4,5},{5,4},{6,7},{7,6},{8,9},{9,8},{10,11... | collective-permute-start | bytes 1179656 | tf_op jit(solution)/shard_map/ppermute | solution.py:284
  13.7 11.6 %collective-permute-start.3 = (bf16[128,1536]{1,0:T(8,128)(2,1)S(1)}, bf16[128,1536]{1,0:T(8,128)(2,1)S(1)}, u32[]{:S(2)}, u32[]{:S(2)}) collective-permute-start(bf16[128,1536]{1,0:T(8,128)(2,1)S(1)} %get-tuple-element.210), channel_id=1, source_target_pairs={{0,2},{1,3},{2,0},{3,1},{4,6},{5,7},{6,4},{7,5},{8,10},{9,11},{10,... | collective-permute-start | bytes 1179656 | tf_op jit(solution)/shard_map/ppermute | solution.py:287
  21.5 15.9 %collective-permute-start.4 = (bf16[128,1536]{1,0:T(8,128)(2,1)S(1)}, bf16[128,1536]{1,0:T(8,128)(2,1)S(1)}, u32[]{:S(2)}, u32[]{:S(2)}) collective-permute-start(bf16[128,1536]{1,0:T(8,128)(2,1)S(1)} %get-tuple-element.213), channel_id=1, source_target_pairs={{0,2},{1,3},{2,0},{3,1},{4,6},{5,7},{6,4},{7,5},{8,10},{9,11},{10,... | collective-permute-start | bytes 1179656 | tf_op jit(solution)/shard_map/ppermute | solution.py:287
  22.1 15.3 %collective-permute-start.5 = (bf16[128,1536]{1,0:T(8,128)(2,1)S(1)}, bf16[128,1536]{1,0:T(8,128)(2,1)S(1)}, u32[]{:S(2)}, u32[]{:S(2)}) collective-permute-start(bf16[128,1536]{1,0:T(8,128)(2,1)S(1)} %get-tuple-element.214), channel_id=1, source_target_pairs={{0,1},{1,0},{2,3},{3,2},{4,5},{5,4},{6,7},{7,6},{8,9},{9,8},{10,11... | collective-permute-start | bytes 1179656 | tf_op jit(solution)/shard_map/ppermute | solution.py:284
  25.3 4.1 %collective-permute-start.6 = (bf16[96,1536]{1,0:T(8,128)(2,1)S(1)}, bf16[96,1536]{1,0:T(8,128)(2,1)S(1)}, u32[]{:S(2)}, u32[]{:S(2)}) collective-permute-start(bf16[96,1536]{1,0:T(8,128)(2,1)S(1)} %get-tuple-element.408), channel_id=1, source_target_pairs={{0,16},{16,0},{1,17},{17,1},{2,18},{18,2},{3,19},{19,3},{4,20},{20... | collective-permute-start | bytes 884744 | tf_op jit(solution)/shard_map/ppermute | solution.py:290
  25.4 4.0 %collective-permute-start.7 = (bf16[96,1536]{1,0:T(8,128)(2,1)S(1)}, bf16[96,1536]{1,0:T(8,128)(2,1)S(1)}, u32[]{:S(2)}, u32[]{:S(2)}) collective-permute-start(bf16[96,1536]{1,0:T(8,128)(2,1)S(1)} %get-tuple-element.407), channel_id=1, source_target_pairs={{0,16},{16,0},{1,17},{17,1},{2,18},{18,2},{3,19},{19,3},{4,20},{20... | collective-permute-start | bytes 884744 | tf_op jit(solution)/shard_map/ppermute | solution.py:290
  27.7 46.1 %collective-permute-start.17 = (bf16[256,1536]{1,0:T(8,128)(2,1)S(1)}, bf16[256,1536]{1,0:T(8,128)(2,1)S(1)}, u32[]{:S(2)}, u32[]{:S(2)}) collective-permute-start(bf16[256,1536]{1,0:T(8,128)(2,1)S(1)} %collective-permute-done.1.mine_ref), channel_id=1, source_target_pairs={{0,4},{4,8},{8,12},{12,0},{1,5},{5,9},{9,13},{13,1},{2,6},{6,10},{... | collective-permute-start | bytes 2359304 | tf_op jit(solution)/shard_map/ppermute | solution.py:293
  32.2 20.5 %collective-permute-start.11 = (bf16[128,3072]{1,0:T(8,128)(2,1)S(1)}, bf16[128,3072]{1,0:T(8,128)(2,1)S(1)}, u32[]{:S(2)}, u32[]{:S(2)}) collective-permute-start(bf16[128,3072]{1,0:T(8,128)(2,1)S(1)} %get-tuple-element.226), channel_id=1, source_target_pairs={{0,1},{1,0},{2,3},{3,2},{4,5},{5,4},{6,7},{7,6},{8,9},{9,8},{10,11... | collective-permute-start | bytes 2359304 | tf_op jit(solution)/shard_map/ppermute | solution.py:284
  35.4 20.5 %collective-permute-start.12 = (bf16[128,3072]{1,0:T(8,128)(2,1)S(1)}, bf16[128,3072]{1,0:T(8,128)(2,1)S(1)}, u32[]{:S(2)}, u32[]{:S(2)}) collective-permute-start(bf16[128,3072]{1,0:T(8,128)(2,1)S(1)} %get-tuple-element.229), channel_id=1, source_target_pairs={{0,2},{1,3},{2,0},{3,1},{4,6},{5,7},{6,4},{7,5},{8,10},{9,11},{10,... | collective-permute-start | bytes 2359304 | tf_op jit(solution)/shard_map/ppermute | solution.py:287
  37.7 26.7 %collective-permute-start.9 = (bf16[64,3072]{1,0:T(8,128)(2,1)S(1)}, bf16[64,3072]{1,0:T(8,128)(2,1)S(1)}, u32[]{:S(2)}, u32[]{:S(2)}) collective-permute-start(bf16[64,3072]{1,0:T(8,128)(2,1)S(1)} %get-tuple-element.237), channel_id=1, source_target_pairs={{0,2},{1,3},{2,0},{3,1},{4,6},{5,7},{6,4},{7,5},{8,10},{9,11},{10,... | collective-permute-start | bytes 1179656 | tf_op jit(solution)/shard_map/ppermute | solution.py:287
  37.8 26.5 %collective-permute-start.10 = (bf16[64,3072]{1,0:T(8,128)(2,1)S(1)}, bf16[64,3072]{1,0:T(8,128)(2,1)S(1)}, u32[]{:S(2)}, u32[]{:S(2)}) collective-permute-start(bf16[64,3072]{1,0:T(8,128)(2,1)S(1)} %get-tuple-element.239), channel_id=1, source_target_pairs={{0,1},{1,0},{2,3},{3,2},{4,5},{5,4},{6,7},{7,6},{8,9},{9,8},{10,11... | collective-permute-start | bytes 1179656 | tf_op jit(solution)/shard_map/ppermute | solution.py:284
  56.8 16.0 %collective-permute-start.15 = (bf16[64,3072]{1,0:T(8,128)(2,1)S(1)}, bf16[64,3072]{1,0:T(8,128)(2,1)S(1)}, u32[]{:S(2)}, u32[]{:S(2)}) collective-permute-start(bf16[64,3072]{1,0:T(8,128)(2,1)S(1)} %get-tuple-element.244), channel_id=1, source_target_pairs={{0,2},{1,3},{2,0},{3,1},{4,6},{5,7},{6,4},{7,5},{8,10},{9,11},{10,... | collective-permute-start | bytes 1179656 | tf_op jit(solution)/shard_map/ppermute | solution.py:287
  58.8 14.0 %collective-permute-start.16 = (bf16[64,3072]{1,0:T(8,128)(2,1)S(1)}, bf16[64,3072]{1,0:T(8,128)(2,1)S(1)}, u32[]{:S(2)}, u32[]{:S(2)}) collective-permute-start(bf16[64,3072]{1,0:T(8,128)(2,1)S(1)} %get-tuple-element.246), channel_id=1, source_target_pairs={{0,1},{1,0},{2,3},{3,2},{4,5},{5,4},{6,7},{7,6},{8,9},{9,8},{10,11... | collective-permute-start | bytes 1179656 | tf_op jit(solution)/shard_map/ppermute | solution.py:284
  65.4 15.8 %collective-permute-start.13 = (bf16[64,3072]{1,0:T(8,128)(2,1)S(1)}, bf16[64,3072]{1,0:T(8,128)(2,1)S(1)}, u32[]{:S(2)}, u32[]{:S(2)}) collective-permute-start(bf16[64,3072]{1,0:T(8,128)(2,1)S(1)} %get-tuple-element.260.refs_0_), channel_id=1, source_target_pairs={{0,2},{1,3},{2,0},{3,1},{4,6},{5,7},{6,4},{7,5},{8,10},{9,11},{10,... | collective-permute-start | bytes 1179656 | tf_op jit(solution)/shard_map/ppermute | solution.py:287
  67.4 15.3 %collective-permute-start.14 = (bf16[64,3072]{1,0:T(8,128)(2,1)S(1)}, bf16[64,3072]{1,0:T(8,128)(2,1)S(1)}, u32[]{:S(2)}, u32[]{:S(2)}) collective-permute-start(bf16[64,3072]{1,0:T(8,128)(2,1)S(1)} %get-tuple-element.262.refs_2_), channel_id=1, source_target_pairs={{0,1},{1,0},{2,3},{3,2},{4,5},{5,4},{6,7},{7,6},{8,9},{9,8},{10,11... | collective-permute-start | bytes 1179656 | tf_op jit(solution)/shard_map/ppermute | solution.py:284
  73.8 9.9 %collective-permute-start.22 = (bf16[128,1536]{1,0:T(8,128)(2,1)S(1)}, bf16[128,1536]{1,0:T(8,128)(2,1)S(1)}, u32[]{:S(2)}, u32[]{:S(2)}) collective-permute-start(bf16[128,1536]{1,0:T(8,128)(2,1)S(1)} %get-tuple-element.406), channel_id=1, source_target_pairs={{0,16},{16,0},{1,17},{17,1},{2,18},{18,2},{3,19},{19,3},{4,20},{20... | collective-permute-start | bytes 1179656 | tf_op jit(solution)/shard_map/ppermute | solution.py:290
  73.9 11.8 %collective-permute-start.23 = (bf16[128,1536]{1,0:T(8,128)(2,1)S(1)}, bf16[128,1536]{1,0:T(8,128)(2,1)S(1)}, u32[]{:S(2)}, u32[]{:S(2)}) collective-permute-start(bf16[128,1536]{1,0:T(8,128)(2,1)S(1)} %get-tuple-element.405), channel_id=1, source_target_pairs={{0,16},{16,0},{1,17},{17,1},{2,18},{18,2},{3,19},{19,3},{4,20},{20... | collective-permute-start | bytes 1179656 | tf_op jit(solution)/shard_map/ppermute | solution.py:290
  74.4 18.4 %collective-permute-start.20 = (bf16[64,3072]{1,0:T(8,128)(2,1)S(1)}, bf16[64,3072]{1,0:T(8,128)(2,1)S(1)}, u32[]{:S(2)}, u32[]{:S(2)}) collective-permute-start(bf16[64,3072]{1,0:T(8,128)(2,1)S(1)} %get-tuple-element.278.refs_0_), channel_id=1, source_target_pairs={{0,2},{1,3},{2,0},{3,1},{4,6},{5,7},{6,4},{7,5},{8,10},{9,11},{10,... | collective-permute-start | bytes 1179656 | tf_op jit(solution)/shard_map/ppermute | solution.py:287
  81.2 12.1 %collective-permute-start.21 = (bf16[64,3072]{1,0:T(8,128)(2,1)S(1)}, bf16[64,3072]{1,0:T(8,128)(2,1)S(1)}, u32[]{:S(2)}, u32[]{:S(2)}) collective-permute-start(bf16[64,3072]{1,0:T(8,128)(2,1)S(1)} %get-tuple-element.280.refs_2_), channel_id=1, source_target_pairs={{0,1},{1,0},{2,3},{3,2},{4,5},{5,4},{6,7},{7,6},{8,9},{9,8},{10,11... | collective-permute-start | bytes 1179656 | tf_op jit(solution)/shard_map/ppermute | solution.py:284
  83.1 27.0 %collective-permute-start.18 = (bf16[128,3072]{1,0:T(8,128)(2,1)S(1)}, bf16[128,3072]{1,0:T(8,128)(2,1)S(1)}, u32[]{:S(2)}, u32[]{:S(2)}) collective-permute-start(bf16[128,3072]{1,0:T(8,128)(2,1)S(1)} %get-tuple-element.284.refs_0_), channel_id=1, source_target_pairs={{0,1},{1,0},{2,3},{3,2},{4,5},{5,4},{6,7},{7,6},{8,9},{9,8},{10,11... | collective-permute-start | bytes 2359304 | tf_op jit(solution)/shard_map/ppermute | solution.py:284
  83.7 26.4 %collective-permute-start.19 = (bf16[128,3072]{1,0:T(8,128)(2,1)S(1)}, bf16[128,3072]{1,0:T(8,128)(2,1)S(1)}, u32[]{:S(2)}, u32[]{:S(2)}) collective-permute-start(bf16[128,3072]{1,0:T(8,128)(2,1)S(1)} %get-tuple-element.286.refs_2_), channel_id=1, source_target_pairs={{0,2},{1,3},{2,0},{3,1},{4,6},{5,7},{6,4},{7,5},{8,10},{9,11},{10,... | collective-permute-start | bytes 2359304 | tf_op jit(solution)/shard_map/ppermute | solution.py:287
  93.3 17.6 %collective-permute-start.24 = (bf16[256,1536]{1,0:T(8,128)(2,1)S(1)}, bf16[256,1536]{1,0:T(8,128)(2,1)S(1)}, u32[]{:S(2)}, u32[]{:S(2)}) collective-permute-start(bf16[256,1536]{1,0:T(8,128)(2,1)S(1)} %collective-permute-done.17.mine_ref), channel_id=1, source_target_pairs={{0,4},{4,8},{8,12},{12,0},{1,5},{5,9},{9,13},{13,1},{2,6},{6,10},{... | collective-permute-start | bytes 2359304 | tf_op jit(solution)/shard_map/ppermute | solution.py:293
  95.4 31.5 %collective-permute-start.28 = (bf16[128,3072]{1,0:T(8,128)(2,1)S(1)}, bf16[128,3072]{1,0:T(8,128)(2,1)S(1)}, u32[]{:S(2)}, u32[]{:S(2)}) collective-permute-start(bf16[128,3072]{1,0:T(8,128)(2,1)S(1)} %get-tuple-element.306.refs_0_), channel_id=1, source_target_pairs={{0,1},{1,0},{2,3},{3,2},{4,5},{5,4},{6,7},{7,6},{8,9},{9,8},{10,11... | collective-permute-start | bytes 2359304 | tf_op jit(solution)/shard_map/ppermute | solution.py:284
  97.0 30.0 %collective-permute-start.29 = (bf16[128,3072]{1,0:T(8,128)(2,1)S(1)}, bf16[128,3072]{1,0:T(8,128)(2,1)S(1)}, u32[]{:S(2)}, u32[]{:S(2)}) collective-permute-start(bf16[128,3072]{1,0:T(8,128)(2,1)S(1)} %get-tuple-element.308.refs_2_), channel_id=1, source_target_pairs={{0,2},{1,3},{2,0},{3,1},{4,6},{5,7},{6,4},{7,5},{8,10},{9,11},{10,... | collective-permute-start | bytes 2359304 | tf_op jit(solution)/shard_map/ppermute | solution.py:287
  111.0 3.9 %collective-permute-start.26 = (bf16[128,1536]{1,0:T(8,128)(2,1)S(1)}, bf16[128,1536]{1,0:T(8,128)(2,1)S(1)}, u32[]{:S(2)}, u32[]{:S(2)}) collective-permute-start(bf16[128,1536]{1,0:T(8,128)(2,1)S(1)} %get-tuple-element.403), channel_id=1, source_target_pairs={{0,16},{16,0},{1,17},{17,1},{2,18},{18,2},{3,19},{19,3},{4,20},{20... | collective-permute-start | bytes 1179656 | tf_op jit(solution)/shard_map/ppermute | solution.py:290
  111.5 32.4 %collective-permute-start.32 = (bf16[128,3072]{1,0:T(8,128)(2,1)}, bf16[128,3072]{1,0:T(8,128)(2,1)S(1)}, u32[]{:S(2)}, u32[]{:S(2)}) collective-permute-start(bf16[128,3072]{1,0:T(8,128)(2,1)} %get-tuple-element.314), channel_id=1, source_target_pairs={{0,1},{1,0},{2,3},{3,2},{4,5},{5,4},{6,7},{7,6},{8,9},{9,8},{10,11... | collective-permute-start | bytes 2359304 | tf_op jit(solution)/shard_map/ppermute | solution.py:284
  113.0 30.9 %collective-permute-start.33 = (bf16[128,3072]{1,0:T(8,128)(2,1)}, bf16[128,3072]{1,0:T(8,128)(2,1)S(1)}, u32[]{:S(2)}, u32[]{:S(2)}) collective-permute-start(bf16[128,3072]{1,0:T(8,128)(2,1)} %get-tuple-element.315), channel_id=1, source_target_pairs={{0,2},{1,3},{2,0},{3,1},{4,6},{5,7},{6,4},{7,5},{8,10},{9,11},{10,... | collective-permute-start | bytes 2359304 | tf_op jit(solution)/shard_map/ppermute | solution.py:287
  127.7 33.0 %collective-permute-start.30 = (bf16[128,3072]{1,0:T(8,128)(2,1)}, bf16[128,3072]{1,0:T(8,128)(2,1)S(1)}, u32[]{:S(2)}, u32[]{:S(2)}) collective-permute-start(bf16[128,3072]{1,0:T(8,128)(2,1)} %get-tuple-element.312), channel_id=1, source_target_pairs={{0,1},{1,0},{2,3},{3,2},{4,5},{5,4},{6,7},{7,6},{8,9},{9,8},{10,11... | collective-permute-start | bytes 2359304 | tf_op jit(solution)/shard_map/ppermute | solution.py:284
  129.2 31.5 %collective-permute-start.31 = (bf16[128,3072]{1,0:T(8,128)(2,1)}, bf16[128,3072]{1,0:T(8,128)(2,1)S(1)}, u32[]{:S(2)}, u32[]{:S(2)}) collective-permute-start(bf16[128,3072]{1,0:T(8,128)(2,1)} %get-tuple-element.313), channel_id=1, source_target_pairs={{0,2},{1,3},{2,0},{3,1},{4,6},{5,7},{6,4},{7,5},{8,10},{9,11},{10,... | collective-permute-start | bytes 2359304 | tf_op jit(solution)/shard_map/ppermute | solution.py:287
  133.8 31.3 %collective-permute-start.42 = (f32[128,1536]{1,0:T(8,128)S(1)}, f32[128,1536]{1,0:T(8,128)S(1)}, u32[]{:S(2)}, u32[]{:S(2)}) collective-permute-start(f32[128,1536]{1,0:T(8,128)S(1)} %get-tuple-element.318), channel_id=1, source_target_pairs={{0,16},{16,0},{1,17},{17,1},{2,18},{18,2},{3,19},{19,3},{4,20},{20... | collective-permute-start | bytes 2359304 | tf_op jit(solution)/shard_map/ppermute | solution.py:290
  146.7 20.5 %collective-permute-start.36 = (bf16[64,3072]{1,0:T(8,128)(2,1)S(1)}, bf16[64,3072]{1,0:T(8,128)(2,1)S(1)}, u32[]{:S(2)}, u32[]{:S(2)}) collective-permute-start(bf16[64,3072]{1,0:T(8,128)(2,1)S(1)} %get-tuple-element.327), channel_id=1, source_target_pairs={{0,2},{1,3},{2,0},{3,1},{4,6},{5,7},{6,4},{7,5},{8,10},{9,11},{10,... | collective-permute-start | bytes 1179656 | tf_op jit(solution)/shard_map/ppermute | solution.py:287
  148.7 20.4 %collective-permute-start.37 = (bf16[64,3072]{1,0:T(8,128)(2,1)S(1)}, bf16[64,3072]{1,0:T(8,128)(2,1)S(1)}, u32[]{:S(2)}, u32[]{:S(2)}) collective-permute-start(bf16[64,3072]{1,0:T(8,128)(2,1)S(1)} %get-tuple-element.329), channel_id=1, source_target_pairs={{0,1},{1,0},{2,3},{3,2},{4,5},{5,4},{6,7},{7,6},{8,9},{9,8},{10,11... | collective-permute-start | bytes 1179656 | tf_op jit(solution)/shard_map/ppermute | solution.py:284
  161.6 12.3 %collective-permute-start.34 = (bf16[64,3072]{1,0:T(8,128)(2,1)S(1)}, bf16[64,3072]{1,0:T(8,128)(2,1)S(1)}, u32[]{:S(2)}, u32[]{:S(2)}) collective-permute-start(bf16[64,3072]{1,0:T(8,128)(2,1)S(1)} %get-tuple-element.336), channel_id=1, source_target_pairs={{0,2},{1,3},{2,0},{3,1},{4,6},{5,7},{6,4},{7,5},{8,10},{9,11},{10,... | collective-permute-start | bytes 1179656 | tf_op jit(solution)/shard_map/ppermute | solution.py:287
  163.6 14.0 %collective-permute-start.35 = (bf16[64,3072]{1,0:T(8,128)(2,1)S(1)}, bf16[64,3072]{1,0:T(8,128)(2,1)S(1)}, u32[]{:S(2)}, u32[]{:S(2)}) collective-permute-start(bf16[64,3072]{1,0:T(8,128)(2,1)S(1)} %get-tuple-element.338), channel_id=1, source_target_pairs={{0,1},{1,0},{2,3},{3,2},{4,5},{5,4},{6,7},{7,6},{8,9},{9,8},{10,11... | collective-permute-start | bytes 1179656 | tf_op jit(solution)/shard_map/ppermute | solution.py:284
  165.4 33.6 %collective-permute-start.43 = (f32[128,1536]{1,0:T(8,128)S(1)}, f32[128,1536]{1,0:T(8,128)S(1)}, u32[]{:S(2)}, u32[]{:S(2)}) collective-permute-start(f32[128,1536]{1,0:T(8,128)S(1)} %add.3), channel_id=1, source_target_pairs={{0,4},{4,8},{8,12},{12,0},{1,5},{5,9},{9,13},{13,1},{2,6},{6,10},{... | collective-permute-start | bytes 2359304 | tf_op jit(solution)/shard_map/ppermute | solution.py:293
  170.1 12.3 %collective-permute-start.40 = (bf16[64,3072]{1,0:T(8,128)(2,1)S(1)}, bf16[64,3072]{1,0:T(8,128)(2,1)S(1)}, u32[]{:S(2)}, u32[]{:S(2)}) collective-permute-start(bf16[64,3072]{1,0:T(8,128)(2,1)S(1)} %get-tuple-element.351.refs_0_), channel_id=1, source_target_pairs={{0,2},{1,3},{2,0},{3,1},{4,6},{5,7},{6,4},{7,5},{8,10},{9,11},{10,... | collective-permute-start | bytes 1179656 | tf_op jit(solution)/shard_map/ppermute | solution.py:287
  172.1 13.9 %collective-permute-start.41 = (bf16[64,3072]{1,0:T(8,128)(2,1)S(1)}, bf16[64,3072]{1,0:T(8,128)(2,1)S(1)}, u32[]{:S(2)}, u32[]{:S(2)}) collective-permute-start(bf16[64,3072]{1,0:T(8,128)(2,1)S(1)} %get-tuple-element.353.refs_2_), channel_id=1, source_target_pairs={{0,1},{1,0},{2,3},{3,2},{4,5},{5,4},{6,7},{7,6},{8,9},{9,8},{10,11... | collective-permute-start | bytes 1179656 | tf_op jit(solution)/shard_map/ppermute | solution.py:284
  178.5 20.5 %collective-permute-start.38 = (bf16[64,3072]{1,0:T(8,128)(2,1)S(1)}, bf16[64,3072]{1,0:T(8,128)(2,1)S(1)}, u32[]{:S(2)}, u32[]{:S(2)}) collective-permute-start(bf16[64,3072]{1,0:T(8,128)(2,1)S(1)} %get-tuple-element.361.refs_0_), channel_id=1, source_target_pairs={{0,2},{1,3},{2,0},{3,1},{4,6},{5,7},{6,4},{7,5},{8,10},{9,11},{10,... | collective-permute-start | bytes 1179656 | tf_op jit(solution)/shard_map/ppermute | solution.py:287
  180.5 18.5 %collective-permute-start.39 = (bf16[64,3072]{1,0:T(8,128)(2,1)S(1)}, bf16[64,3072]{1,0:T(8,128)(2,1)S(1)}, u32[]{:S(2)}, u32[]{:S(2)}) collective-permute-start(bf16[64,3072]{1,0:T(8,128)(2,1)S(1)} %get-tuple-element.363.refs_2_), channel_id=1, source_target_pairs={{0,1},{1,0},{2,3},{3,2},{4,5},{5,4},{6,7},{7,6},{8,9},{9,8},{10,11... | collective-permute-start | bytes 1179656 | tf_op jit(solution)/shard_map/ppermute | solution.py:284
  186.4 24.9 %collective-permute-start.46 = (bf16[128,3072]{1,0:T(8,128)(2,1)S(1)}, bf16[128,3072]{1,0:T(8,128)(2,1)S(1)}, u32[]{:S(2)}, u32[]{:S(2)}) collective-permute-start(bf16[128,3072]{1,0:T(8,128)(2,1)S(1)} %get-tuple-element.367.refs_0_), channel_id=1, source_target_pairs={{0,1},{1,0},{2,3},{3,2},{4,5},{5,4},{6,7},{7,6},{8,9},{9,8},{10,11... | collective-permute-start | bytes 2359304 | tf_op jit(solution)/shard_map/ppermute | solution.py:284
  187.9 23.3 %collective-permute-start.47 = (bf16[128,3072]{1,0:T(8,128)(2,1)S(1)}, bf16[128,3072]{1,0:T(8,128)(2,1)S(1)}, u32[]{:S(2)}, u32[]{:S(2)}) collective-permute-start(bf16[128,3072]{1,0:T(8,128)(2,1)S(1)} %get-tuple-element.369.refs_2_), channel_id=1, source_target_pairs={{0,2},{1,3},{2,0},{3,1},{4,6},{5,7},{6,4},{7,5},{8,10},{9,11},{10,... | collective-permute-start | bytes 2359304 | tf_op jit(solution)/shard_map/ppermute | solution.py:287
  199.4 25.3 %collective-permute-start.44 = (bf16[128,3072]{1,0:T(8,128)(2,1)S(1)}, bf16[128,3072]{1,0:T(8,128)(2,1)S(1)}, u32[]{:S(2)}, u32[]{:S(2)}) collective-permute-start(bf16[128,3072]{1,0:T(8,128)(2,1)S(1)} %get-tuple-element.381.refs_0_), channel_id=1, source_target_pairs={{0,1},{1,0},{2,3},{3,2},{4,5},{5,4},{6,7},{7,6},{8,9},{9,8},{10,11... | collective-permute-start | bytes 2359304 | tf_op jit(solution)/shard_map/ppermute | solution.py:284
  200.0 24.7 %collective-permute-start.45 = (bf16[128,3072]{1,0:T(8,128)(2,1)S(1)}, bf16[128,3072]{1,0:T(8,128)(2,1)S(1)}, u32[]{:S(2)}, u32[]{:S(2)}) collective-permute-start(bf16[128,3072]{1,0:T(8,128)(2,1)S(1)} %get-tuple-element.383.refs_2_), channel_id=1, source_target_pairs={{0,2},{1,3},{2,0},{3,1},{4,6},{5,7},{6,4},{7,5},{8,10},{9,11},{10,... | collective-permute-start | bytes 2359304 | tf_op jit(solution)/shard_map/ppermute | solution.py:287
  217.3 13.0 %collective-permute-start.52 = (bf16[128,1536]{1,0:T(8,128)(2,1)S(1)}, bf16[128,1536]{1,0:T(8,128)(2,1)S(1)}, u32[]{:S(2)}, u32[]{:S(2)}) collective-permute-start(bf16[128,1536]{1,0:T(8,128)(2,1)S(1)} %add.4), channel_id=1, source_target_pairs={{0,4},{4,8},{8,12},{12,0},{1,5},{5,9},{9,13},{13,1},{2,6},{6,10},{... | collective-permute-start | bytes 1179656 | tf_op jit(solution)/shard_map/ppermute | solution.py:293
  228.6 20.5 %collective-permute-start.27 = (f32[128,1536]{1,0:T(8,128)}, f32[128,1536]{1,0:T(8,128)S(1)}, u32[]{:S(2)}, u32[]{:S(2)}) collective-permute-start(f32[128,1536]{1,0:T(8,128)} %get-tuple-element.305), channel_id=1, source_target_pairs={{0,16},{16,0},{1,17},{17,1},{2,18},{18,2},{3,19},{19,3},{4,20},{20... | collective-permute-start | bytes 2359304 | tf_op jit(solution)/shard_map/ppermute | solution.py:290
  231.4 17.8 %collective-permute-start.53 = (bf16[128,1536]{1,0:T(8,128)(2,1)S(1)}, bf16[128,1536]{1,0:T(8,128)(2,1)S(1)}, u32[]{:S(2)}, u32[]{:S(2)}) collective-permute-start(bf16[128,1536]{1,0:T(8,128)(2,1)S(1)} %add.5), channel_id=1, source_target_pairs={{0,4},{4,8},{8,12},{12,0},{1,5},{5,9},{9,13},{13,1},{2,6},{6,10},{... | collective-permute-start | bytes 1179656 | tf_op jit(solution)/shard_map/ppermute | solution.py:293
  (37 other events, 270.4 us)
